TPU v7x, 256 devices: a whole 4x4x8 slice. The times are simulated.
256 devices in a mesh: dp: 2 (over core), dom: 128 (over y, z, x).
Axes of the slice: x: 4, y: 4, z: 8, core: 2. Of those that a mesh axis runs over, the one named last changes fastest.
Arguments:
- node_latent: bfloat16 [65536, 512], P(('dp', 'dom')), parts along dimension 0, may hold values from -6 to 6
- edge_latent: bfloat16 [524288, 512], P(('dp', 'dom')), parts along dimension 0, may hold values from -6 to 6
- edge_sender: int32 [524288], P(('dp', 'dom')), parts along dimension 0, may hold values from 0 to 767, as said below
- edge_receiver: int32 [524288], P(('dp', 'dom')), parts along dimension 0, may hold values from 0 to 255
- edge_mask: int32 [524288], P(('dp', 'dom')), parts along dimension 0, may hold values from 0 to 1, as said below
- send_list: int32 [256, 128, 4], P(('dp', 'dom')), parts along dimension 0, may hold values from -1 to 255, as said below
- edge_in: bfloat16 [2, 3, 512, 512], replicated, may hold values from -0.15625 to 0.15625
- edge_out: bfloat16 [2, 512, 512], replicated, may hold values from -0.25 to 0.25
- node_in: bfloat16 [2, 2, 512, 512], replicated, may hold values from -0.1875 to 0.1875
- node_out: bfloat16 [2, 512, 512], replicated, may hold values from -0.25 to 0.25
- biases: float32 [2, 4, 512], replicated, may hold values from -3 to 3
- ln_gain: float32 [2, 2, 512], replicated, may hold values from 0.5 to 1.5
- ln_shift: float32 [2, 2, 512], replicated, may hold values from -2 to 2
Outputs:
- node_state: bfloat16 [65536, 512], P(('dp', 'dom')), parts along dimension 0
- edge_state: bfloat16 [524288, 512], P(('dp', 'dom')), parts along dimension 0
There are 2 independent parts, one for each index of `dp`. A program takes and returns all parts, laid end to end along the dimension named above; an argument that names none is the same for every part. Nothing has to cross between parts.
Inputs may be any that keep to these rules, and one draw needn't show every extreme that they name: send_list[p, r, k] is a local node index of partition p for k below the count of the pair (p, r) and -1 from there on; a partition sends nothing to itself, every other pair has a count of 1 to 4, and in every draw some partition receives 4 from every other one. `edge_sender`: within each partition's 2048 slots, the first half have local senders (below 256); the second half have senders 256 + p * 4 + k naming a halo slot whose send_list[p, r, k] is not -1, with r the edge's partition. `edge_mask`: within each half of a partition's slots the real edges come first; every halo slot that holds a node is the sender of some real edge.
All inputs are finite; a program needn't handle non-finite values.
Results may differ from a plain program's by a relative error of at most 0.013.
Values may be sent and summed in bfloat16 or wider, within the bound.
A program may use at most 128 MiB of HBM per device.

v0:
```python
import jax
import jax.numpy as jnp
from jax import lax
from jax.sharding import PartitionSpec as P


def layer_norm(values, gain_vec, shift_vec):
    row_mean = jnp.mean(values, axis=-1, keepdims=True)
    centered = values - row_mean
    variance = jnp.mean(centered * centered, axis=-1, keepdims=True)
    return centered * lax.rsqrt(variance + 1e-05) * gain_vec + shift_vec


def edge_message(
    latent,
    sender_part,
    receiver_part,
    w_edge,
    w_output,
    bias_hidden,
    bias_output,
    gain_vec,
    shift_vec,
):
    hidden = jnp.dot(latent, w_edge, preferred_element_type=jnp.float32)
    hidden = (
        hidden + sender_part.astype(jnp.float32) + receiver_part.astype(jnp.float32) + bias_hidden
    )
    activated = jax.nn.silu(hidden).astype(jnp.bfloat16)
    projected = jnp.dot(activated, w_output, preferred_element_type=jnp.float32) + bias_output
    return layer_norm(projected, gain_vec, shift_vec).astype(jnp.bfloat16)


def local(
    node_latent,
    edge_latent,
    edge_sender,
    edge_receiver,
    edge_mask,
    send_list,
    edge_in,
    edge_out,
    node_in,
    node_out,
    biases,
    ln_gain,
    ln_shift,
):
    n_local = node_latent.shape[0]
    n_edges = edge_latent.shape[0]
    half_edges = n_edges // 2
    feature_width = node_latent.shape[1]
    send_rows = send_list[0]
    halo_count = send_rows.shape[0] * send_rows.shape[1]
    present = send_rows >= 0
    pick_rows = jnp.maximum(send_rows, 0)
    live_edge = edge_mask > 0
    node_columns = jnp.arange(n_local, dtype=jnp.int32)[None, :]
    halo_columns = jnp.arange(halo_count, dtype=jnp.int32)[None, :] + n_local
    receive_table = (edge_receiver[:, None] == node_columns).astype(jnp.bfloat16)
    local_table = (edge_sender[:half_edges, None] == node_columns).astype(jnp.bfloat16)
    remote_table = (edge_sender[half_edges:, None] == halo_columns).astype(jnp.bfloat16)
    zero_bf = jnp.zeros((), jnp.bfloat16)
    node_state = node_latent
    edge_state = edge_latent
    for layer_index in range(edge_in.shape[0]):
        w_edge = edge_in[layer_index, 0]
        w_send = edge_in[layer_index, 1]
        w_recv = edge_in[layer_index, 2]
        w_output = edge_out[layer_index]
        bias_hidden = biases[layer_index, 0]
        bias_output = biases[layer_index, 1]
        gain_edge = ln_gain[layer_index, 0]
        shift_edge = ln_shift[layer_index, 0]
        recv_proj = jnp.dot(node_state, w_recv, preferred_element_type=jnp.float32).astype(
            jnp.bfloat16
        )
        outgoing = jnp.where(present[:, :, None], node_state[pick_rows], zero_bf)

        def project(peer_rows, weight_now=w_send):
            return jnp.einsum(
                "pkd,de->pke", peer_rows, weight_now, preferred_element_type=jnp.float32
            ).astype(jnp.bfloat16)

        halo_rows = project(
            lax.all_to_all(outgoing, "dom", split_axis=0, concat_axis=0, tiled=True)
        )
        send_proj = jnp.dot(node_state, w_send, preferred_element_type=jnp.float32).astype(
            jnp.bfloat16
        )
        local_part = jnp.dot(local_table, send_proj, preferred_element_type=jnp.float32)
        remote_part = jnp.dot(
            remote_table, halo_rows.reshape(-1, feature_width), preferred_element_type=jnp.float32
        )
        sender_part = jnp.concatenate([local_part, remote_part], axis=0).astype(jnp.bfloat16)
        receiver_part = jnp.dot(
            receive_table, recv_proj, preferred_element_type=jnp.float32
        ).astype(jnp.bfloat16)
        message = edge_message(
            edge_state,
            sender_part,
            receiver_part,
            w_edge,
            w_output,
            bias_hidden,
            bias_output,
            gain_edge,
            shift_edge,
        )
        message = jnp.where(live_edge[:, None], message, zero_bf)
        edge_state = (edge_state.astype(jnp.float32) + message.astype(jnp.float32)).astype(
            jnp.bfloat16
        )
        aggregated = lax.dot_general(
            receive_table, message, (((0,), (0,)), ((), ())), preferred_element_type=jnp.float32
        ).astype(jnp.bfloat16)
        node_hidden = jnp.dot(
            node_state, node_in[layer_index, 0], preferred_element_type=jnp.float32
        )
        node_hidden = (
            node_hidden
            + jnp.dot(aggregated, node_in[layer_index, 1], preferred_element_type=jnp.float32)
            + biases[layer_index, 2]
        )
        node_act = jax.nn.silu(node_hidden).astype(jnp.bfloat16)
        node_proj = (
            jnp.dot(node_act, node_out[layer_index], preferred_element_type=jnp.float32)
            + biases[layer_index, 3]
        )
        node_state = (
            node_state.astype(jnp.float32)
            + layer_norm(node_proj, ln_gain[layer_index, 1], ln_shift[layer_index, 1])
        ).astype(jnp.bfloat16)
    return (node_state, edge_state)


def solution(mesh):
    in_specs = (
        P(("dp", "dom"), None),
        P(("dp", "dom"), None),
        P(("dp", "dom")),
        P(("dp", "dom")),
        P(("dp", "dom")),
        P(("dp", "dom"), None, None),
        P(),
        P(),
        P(),
        P(),
        P(),
        P(),
        P(),
    )
    out_specs = (P(("dp", "dom"), None), P(("dp", "dom"), None))
    return jax.shard_map(local, mesh=mesh, in_specs=in_specs, out_specs=out_specs, check_vma=False)
```

profile of v0, /device:TPU:2, one launch (start us, length us, event | category | flops | bytes accessed | tf_op | source)
XLA Modules:
  0.0 124.2 jit_solution(5158775708581481911)
XLA Ops:
  0.6 0.7 broadcast_maximum_fusion
  1.3 0.7 compare_bitcast_fusion
  2.0 0.1 copy.25
  2.1 0.1 reshape.106
  2.2 0.0 copy-start.8
  2.3 3.0 %gather_fusion = bf16[512,512]{1,0:T(8,128)(2,1)S(1)} fusion(bf16[256,512]{1,0:T(8,128)(2,1)} %param.13, s32[1024]{0:T(1024)S(1)} %pad_clamp_fusion), kind=kCustom, calls=%fused_computation | custom fusion | bytes 1050624 | tf_op jit(solution)/shard_map/gather | solution.py:78
  5.4 0.1 reshape.105
  5.5 0.1 copy.24
  5.6 1.2 broadcast_select_fusion.1
  6.8 15.4 %all-to-all-start = ((bf16[128,4,512]{2,1,0:T(4,128)(2,1)}), bf16[128,4,512]{2,1,0:T(4,128)(2,1)S(1)}, u32[]{:S(2)}, u32[]{:S(2)}) async-start(bf16[128,4,512]{2,1,0:T(4,128)(2,1)} %broadcast_select_fusion.1), calls=%async_computation | async-start | bytes 1048576 | tf_op jit(solution)/shard_map/all_to_all | solution.py:86
  22.4 2.1 %fusion.63 = f32[256,512]{1,0:T(8,128)} fusion(bf16[256,512]{1,0:T(8,128)(2,1)S(1)} %copy-done, bf16[2,2,512,512]{3,2,1,0:T(8,128)(2,1)} %param.21), kind=kOutput, calls=%fused_computation.69 | convolution fusion | flops 134217728 | bytes 1310720 | tf_op jit(solution)/shard_map/dot_general | solution.py:117
  24.5 2.7 %convolution_convert_fusion.3 = bf16[1024,512]{1,0:T(8,128)(2,1)} fusion(bf16[256,512]{1,0:T(8,128)(2,1)S(1)} %copy-done, s32[1024]{0:T(1024)S(1)} %get-tuple-element.26, bf16[2,3,512,512]{3,2,1,0:T(8,128)(2,1)} %param.19), kind=kOutput, calls=%fused_computation.25 | convolution fusion | flops 403570688 | bytes 1839104 | tf_op jit(solution)/shard_map/dot_general | solution.py:91
  27.3 3.4 %convolution_convert_fusion.1 = bf16[2048,512]{1,0:T(8,128)(2,1)} fusion(bf16[256,512]{1,0:T(8,128)(2,1)S(1)} %copy-done, s32[2048]{0:T(1024)S(1)} %copy-done.13, bf16[2,3,512,512]{3,2,1,0:T(8,128)(2,1)} %param.19), kind=kOutput, calls=%fused_computation.13 | convolution fusion | flops 672792576 | bytes 2891776 | tf_op jit(solution)/shard_map/dot_general | solution.py:96
  30.6 10.3 %all-to-all-done = bf16[128,4,512]{2,1,0:T(4,128)(2,1)S(1)} async-done(((bf16[128,4,512]{2,1,0:T(4,128)(2,1)}), bf16[128,4,512]{2,1,0:T(4,128)(2,1)S(1)}, u32[]{:S(2)}, u32[]{:S(2)}) %all-to-all-start) | async-done | bytes 524320 | tf_op jit(solution)/shard_map/all_to_all | solution.py:86
  40.9 1.5 %convolution_convert_fusion.5 = bf16[128,4,512]{2,0,1:T(8,128)(2,1)S(1)} fusion(bf16[128,4,512]{2,1,0:T(4,128)(2,1)S(1)} %all-to-all-done, bf16[2,3,512,512]{3,2,1,0:T(8,128)(2,1)} %param.19), kind=kOutput, calls=%fused_computation.31 | convolution fusion | flops 268697600 | bytes 1572864 | tf_op jit(solution)/shard_map/pkd,de->pke/dot_general | solution.py:81
  42.4 0.4 copy.27
  42.8 0.1 reshape.102
  43.0 1.8 %fusion.9 = bf16[1024,512]{1,0:T(8,128)(2,1)} fusion(bf16[512,512]{1,0:T(8,128)(2,1)S(1)} %reshape.102, s32[512]{0:T(512)S(1)} %iota_add_fusion, s32[1024]{0:T(1024)S(1)} %get-tuple-element.27), kind=kOutput, calls=%fused_computation.26 | convolution fusion | flops 537919488 | bytes 1579008 | tf_op jit(solution)/shard_map/dot_general | solution.py:92
  44.7 7.5 %add_reduce_fusion.1 = (f32[2048]{0:T(1024)S(1)}, f32[2048,512]{0,1:T(8,128)}) fusion(f32[512]{0:T(512)S(1)} %bitcast.103, bf16[2,512,512]{2,1,0:T(8,128)(2,1)} %param.20, bf16[2048,512]{1,0:T(8,128)(2,1)} %convolution_convert_fusion.1, bf16[2048,512]{1,0:T(8,128)(2,1)S(1)} %copy-done.3, bf16[1024,512]{1,0:T(8,128)(2,1)} %fusion.9, ...), kind=kOutput, calls=%fused_computation.11 | convolution fusion | flops 2163210240 | bytes 11546624 | tf_op jit(solution)/shard_map/dot_general | solution.py:30
  52.3 3.0 %multiply_reduce_fusion.1 = f32[2048]{0:T(1024)S(1)} fusion(f32[2048,512]{0,1:T(8,128)} %get-tuple-element.29, f32[2048]{0:T(1024)S(1)} %broadcast_multiply_fusion.1, f32[512]{0:T(512)S(1)} %bitcast.104), kind=kLoop, calls=%fused_computation.8 | loop fusion | flops 4192256 | bytes 4212736 | tf_op jit(solution)/shard_map/reduce_sum | solution.py:10
  55.2 0.5 copy-done.1
  55.7 1.0 fusion.4
  56.8 4.1 %multiply_convert_fusion.3 = bf16[256,512]{1,0:T(8,128)(2,1)} fusion(f32[256,512]{1,0:T(8,128)} %fusion.63, bf16[2048,512]{0,1:T(8,128)(2,1)S(1)} %fusion.4, s32[2048]{0:T(1024)S(1)} %copy-done.13, bf16[2,2,512,512]{3,2,1,0:T(8,128)(2,1)} %param.21, f32[512]{0:T(512)S(1)} %bitcast.124), kind=kOutput, calls=%fused_computation.85 | convolution fusion | flops 673185792 | bytes 3418112 | tf_op jit(solution)/shard_map/dot_general | solution.py:122
  60.9 1.3 %fusion.110 = (f32[256]{0:T(256)S(1)}, f32[256,512]{1,0:T(8,128)S(1)}) fusion(f32[512]{0:T(512)S(1)} %bitcast.115, bf16[256,512]{1,0:T(8,128)(2,1)} %multiply_convert_fusion.3, bf16[2,512,512]{2,1,0:T(8,128)(2,1)S(1)} %copy-done.6), kind=kOutput, calls=%fused_computation.120 | convolution fusion | flops 134479616 | bytes 1313792 | tf_op jit(solution)/shard_map/dot_general | solution.py:127
  62.3 0.2 multiply_reduce_fusion.3
  62.5 0.2 add_convert_fusion.7
  62.7 2.0 %gather_fusion.1 = bf16[512,512]{1,0:T(8,128)(2,1)S(1)} fusion(bf16[256,512]{1,0:T(8,128)(2,1)S(1)} %add_convert_fusion.7, s32[1024]{0:T(1024)S(1)} %pad_clamp_fusion), kind=kCustom, calls=%fused_computation.1 | custom fusion | bytes 1050624 | tf_op jit(solution)/shard_map/gather | solution.py:78
  64.7 0.1 reshape.113
  64.8 1.1 broadcast_select_fusion
  65.9 7.6 %all-to-all-start.1 = ((bf16[128,4,512]{2,1,0:T(4,128)(2,1)}), bf16[128,4,512]{2,1,0:T(4,128)(2,1)S(1)}, u32[]{:S(2)}, u32[]{:S(2)}) async-start(bf16[128,4,512]{2,1,0:T(4,128)(2,1)} %broadcast_select_fusion), calls=%async_computation.1 | async-start | bytes 1048576 | tf_op jit(solution)/shard_map/all_to_all | solution.py:86
  73.5 2.9 %copy.28 = bf16[2048,512]{0,1:T(8,128)(2,1)S(1)} copy(bf16[2048,512]{1,0:T(8,128)(2,1)} %param.14) | data formatting | bytes 4194304 | tf_op args[1]
  76.5 2.2 %fusion.52 = f32[256,512]{1,0:T(8,128)} fusion(bf16[256,512]{1,0:T(8,128)(2,1)S(1)} %add_convert_fusion.7, bf16[2,2,512,512]{3,2,1,0:T(8,128)(2,1)} %param.21), kind=kOutput, calls=%fused_computation.61 | convolution fusion | flops 134217728 | bytes 1310720 | tf_op jit(solution)/shard_map/dot_general | solution.py:117
  78.6 2.7 %convolution_convert_fusion.2 = bf16[1024,512]{1,0:T(8,128)(2,1)} fusion(bf16[256,512]{1,0:T(8,128)(2,1)S(1)} %add_convert_fusion.7, s32[1024]{0:T(1024)S(1)} %get-tuple-element.26, bf16[2,3,512,512]{3,2,1,0:T(8,128)(2,1)} %param.19), kind=kOutput, calls=%fused_computation.24 | convolution fusion | flops 403570688 | bytes 1839104 | tf_op jit(solution)/shard_map/dot_general | solution.py:91
  81.4 3.4 %convolution_convert_fusion = bf16[2048,512]{1,0:T(8,128)(2,1)} fusion(bf16[256,512]{1,0:T(8,128)(2,1)S(1)} %add_convert_fusion.7, s32[2048]{0:T(1024)S(1)} %copy-done.13, bf16[2,3,512,512]{3,2,1,0:T(8,128)(2,1)} %param.19), kind=kOutput, calls=%fused_computation.12 | convolution fusion | flops 672792576 | bytes 2891776 | tf_op jit(solution)/shard_map/dot_general | solution.py:96
  84.7 6.4 %all-to-all-done.1 = bf16[128,4,512]{2,1,0:T(4,128)(2,1)S(1)} async-done(((bf16[128,4,512]{2,1,0:T(4,128)(2,1)}), bf16[128,4,512]{2,1,0:T(4,128)(2,1)S(1)}, u32[]{:S(2)}, u32[]{:S(2)}) %all-to-all-start.1) | async-done | bytes 524320 | tf_op jit(solution)/shard_map/all_to_all | solution.py:86
  91.1 1.5 %convolution_convert_fusion.4 = bf16[128,4,512]{2,0,1:T(8,128)(2,1)S(1)} fusion(bf16[128,4,512]{2,1,0:T(4,128)(2,1)S(1)} %all-to-all-done.1, bf16[2,3,512,512]{3,2,1,0:T(8,128)(2,1)} %param.19), kind=kOutput, calls=%fused_computation.30 | convolution fusion | flops 268697600 | bytes 1572864 | tf_op jit(solution)/shard_map/pkd,de->pke/dot_general | solution.py:81
  92.6 0.4 copy.30
  93.0 0.9 reshape.103
  93.9 2.8 %fusion.12 = bf16[1024,512]{1,0:T(8,128)(2,1)} fusion(bf16[512,512]{1,0:T(8,128)(2,1)} %reshape.103, s32[512]{0:T(512)S(1)} %iota_add_fusion, s32[1024]{0:T(1024)S(1)} %get-tuple-element.27), kind=kOutput, calls=%fused_computation.27 | convolution fusion | flops 537919488 | bytes 1579008 | tf_op jit(solution)/shard_map/dot_general | solution.py:92
  96.7 8.5 %add_reduce_fusion = (f32[2048]{0:T(1024)S(1)}, f32[2048,512]{0,1:T(8,128)}) fusion(f32[512]{0:T(512)S(1)} %bitcast.107, bf16[2,512,512]{2,1,0:T(8,128)(2,1)} %param.20, bf16[2048,512]{1,0:T(8,128)(2,1)} %convolution_convert_fusion, bf16[1024,512]{1,0:T(8,128)(2,1)} %fusion.12, bf16[1024,512]{1,0:T(8,128)(2,1)} %convolution_convert_fusion.2, ...), kind=kOutput, calls=%fused_computation.10 | convolution fusion | flops 2167404544 | bytes 13643776 | tf_op jit(solution)/shard_map/dot_general | solution.py:30
  105.2 3.0 %multiply_reduce_fusion = f32[2048]{0:T(1024)S(1)} fusion(f32[2048,512]{0,1:T(8,128)} %get-tuple-element.33, f32[2048]{0:T(1024)S(1)} %broadcast_multiply_fusion, f32[512]{0:T(512)S(1)} %bitcast.108), kind=kLoop, calls=%fused_computation.4 | loop fusion | flops 4192256 | bytes 4212736 | tf_op jit(solution)/shard_map/reduce_sum | solution.py:10
  108.2 0.5 copy-done.2
  108.6 6.4 %add_convert_fusion = (bf16[2048,512]{0,1:T(8,128)(2,1)}, bf16[2048,512]{0,1:T(8,128)(2,1)}) fusion(bf16[2048,512]{0,1:T(8,128)(2,1)S(1)} %copy.28, f32[512]{0:T(512)S(1)} %bitcast.118, f32[512]{0:T(512)S(1)} %bitcast.119, f32[2048]{0:T(1024)S(1)} %add_rsqrt_fusion, f32[2048]{0:T(1024)S(1)} %broadcast_multiply_fusion, f32[2048,512]{0,1:T(8,128)} %get-tuple-element.33, ...), kind=kLoop, calls=%fused_computation.2 | loop fusion | flops 23068672 | bytes 14727168 | tf_op jit(solution)/shard_map/convert_element_type | solution.py:111
  115.0 4.1 %copy.31 = bf16[2048,512]{1,0:T(8,128)(2,1)} copy(bf16[2048,512]{0,1:T(8,128)(2,1)} %get-tuple-element.8) | data formatting | bytes 4194304
  119.1 2.5 %multiply_convert_fusion.2 = bf16[256,512]{1,0:T(8,128)(2,1)S(1)} fusion(f32[256,512]{1,0:T(8,128)S(1)} %copy-done.7, bf16[2048,512]{0,1:T(8,128)(2,1)S(1)} %copy-done.5, s32[2048]{0:T(1024)S(1)} %copy-done.13, bf16[2,2,512,512]{3,2,1,0:T(8,128)(2,1)} %param.21, f32[512]{0:T(512)S(1)} %bitcast.122), kind=kOutput, calls=%fused_computation.76 | convolution fusion | flops 673185792 | bytes 3418112 | tf_op jit(solution)/shard_map/dot_general | solution.py:122
  121.6 1.4 %fusion.113 = (f32[256]{0:T(256)S(1)}, f32[256,512]{1,0:T(8,128)S(1)}) fusion(f32[512]{0:T(512)S(1)} %bitcast.114, bf16[256,512]{1,0:T(8,128)(2,1)S(1)} %multiply_convert_fusion.2, bf16[2,512,512]{2,1,0:T(8,128)(2,1)} %param.22), kind=kOutput, calls=%fused_computation.121 | convolution fusion | flops 134479616 | bytes 1313792 | tf_op jit(solution)/shard_map/dot_general | solution.py:127
  123.0 0.2 multiply_reduce_fusion.2
  123.3 0.9 add_convert_fusion.6
  (40 shorter events, 0.2 us)
Async XLA Ops:
  2.2 20.0 %copy-start.8 = (f32[2,4,512]{2,1,0:T(4,128)S(1)}, f32[2,4,512]{2,1,0:T(4,128)}, u32[]{:S(2)}) copy-start(f32[2,4,512]{2,1,0:T(4,128)} %param.23) | copy-start | bytes 49156
  2.2 20.0 %copy-start.10 = (s32[2048]{0:T(1024)S(1)}, s32[2048]{0:T(1024)}, u32[]{:S(2)}) copy-start(s32[2048]{0:T(1024)} %param.15) | copy-start | bytes 24580
  2.3 20.0 %copy-start.11 = (f32[2,2,512]{2,1,0:T(2,128)S(1)}, f32[2,2,512]{2,1,0:T(2,128)}, u32[]{:S(2)}) copy-start(f32[2,2,512]{2,1,0:T(2,128)} %param.25) | copy-start | bytes 24580
  2.3 20.1 %copy-start.12 = (f32[2,2,512]{2,1,0:T(2,128)S(1)}, f32[2,2,512]{2,1,0:T(2,128)}, u32[]{:S(2)}) copy-start(f32[2,2,512]{2,1,0:T(2,128)} %param.24) | copy-start | bytes 24580
  2.3 20.1 %copy-start.9 = (s32[2048]{0:T(1024)S(1)}, s32[2048]{0:T(1024)}, u32[]{:S(2)}) copy-start(s32[2048]{0:T(1024)} %param.17) | copy-start | bytes 24580
  2.3 20.1 %copy-start = (bf16[256,512]{1,0:T(8,128)(2,1)S(1)}, bf16[256,512]{1,0:T(8,128)(2,1)}, u32[]{:S(2)}) copy-start(bf16[256,512]{1,0:T(8,128)(2,1)} %param.13) | copy-start | bytes 786436
  5.3 21.9 %copy-start.13 = (s32[2048]{0:T(1024)S(1)}, s32[2048]{0:T(1024)}, u32[]{:S(2)}) copy-start(s32[2048]{0:T(1024)} %param.16) | copy-start | bytes 24580
  6.8 34.2 %all-to-all-start = ((bf16[128,4,512]{2,1,0:T(4,128)(2,1)}), bf16[128,4,512]{2,1,0:T(4,128)(2,1)S(1)}, u32[]{:S(2)}, u32[]{:S(2)}) async-start(bf16[128,4,512]{2,1,0:T(4,128)(2,1)} %broadcast_select_fusion.1), calls=%async_computation | async-start | bytes 1048576 | tf_op jit(solution)/shard_map/all_to_all | solution.py:86
  30.6 14.1 %copy-start.3 = (bf16[2048,512]{1,0:T(8,128)(2,1)S(1)}, bf16[2048,512]{1,0:T(8,128)(2,1)}, u32[]{:S(2)}) copy-start(bf16[2048,512]{1,0:T(8,128)(2,1)} %param.14) | copy-start | bytes 6291460
  52.3 3.4 %copy-start.1 = (f32[2048,512]{0,1:T(8,128)S(1)}, f32[2048,512]{0,1:T(8,128)}, u32[]{:S(2)}) copy-start(f32[2048,512]{0,1:T(8,128)} %get-tuple-element.29) | copy-start | bytes 12582916
  56.7 4.2 %copy-start.4 = (bf16[2048,512]{0,1:T(8,128)(2,1)}, bf16[2048,512]{0,1:T(8,128)(2,1)S(1)}, u32[]{:S(2)}) copy-start(bf16[2048,512]{0,1:T(8,128)(2,1)S(1)} %fusion.4) | copy-start | bytes 6291460
  56.8 4.2 %copy-start.6 = (bf16[2,512,512]{2,1,0:T(8,128)(2,1)S(1)}, bf16[2,512,512]{2,1,0:T(8,128)(2,1)}, u32[]{:S(2)}) copy-start(bf16[2,512,512]{2,1,0:T(8,128)(2,1)} %param.22) | copy-start | bytes 3145732
  65.9 25.2 %all-to-all-start.1 = ((bf16[128,4,512]{2,1,0:T(4,128)(2,1)}), bf16[128,4,512]{2,1,0:T(4,128)(2,1)S(1)}, u32[]{:S(2)}, u32[]{:S(2)}) async-start(bf16[128,4,512]{2,1,0:T(4,128)(2,1)} %broadcast_select_fusion), calls=%async_computation.1 | async-start | bytes 1048576 | tf_op jit(solution)/shard_map/all_to_all | solution.py:86
  105.2 3.4 %copy-start.2 = (f32[2048,512]{0,1:T(8,128)S(1)}, f32[2048,512]{0,1:T(8,128)}, u32[]{:S(2)}) copy-start(f32[2048,512]{0,1:T(8,128)} %get-tuple-element.29) | copy-start | bytes 12582916
  115.0 4.1 %copy-start.5 = (bf16[2048,512]{0,1:T(8,128)(2,1)S(1)}, bf16[2048,512]{0,1:T(8,128)(2,1)}, u32[]{:S(2)}) copy-start(bf16[2048,512]{0,1:T(8,128)(2,1)} %get-tuple-element.9) | copy-start | bytes 6291460
  115.0 4.1 %copy-start.7 = (f32[256,512]{1,0:T(8,128)S(1)}, f32[256,512]{1,0:T(8,128)}, u32[]{:S(2)}) copy-start(f32[256,512]{1,0:T(8,128)} %fusion.52) | copy-start | bytes 1572868
where the time goes:
time: 125 us; the launch traced here: 124 us
  matrix products  49.4 us (40%)
  starting transfers between devices  23 us (18%)
  other arithmetic  18.6 us (15%)
  waiting for transfers between devices  16.7 us (13%)
  local copies, waits for them, and re-layouts  15.5 us (12%)
    all_to_all x2, starting transfers between devices, local(): lax.all_to_all(outgoing, 'dom', split_axis=0, concat_axis=0, tiled=True)  23 us
    all_to_all x2, waiting for transfers between devices, local(): lax.all_to_all(outgoing, 'dom', split_axis=0, concat_axis=0, tiled=True)  16.7 us
    dot_general x2, matrix products, edge_message(): jnp.dot(activated, w_output, preferred_element_type=jnp.float32)  16 us
    unnamed x30, local copies, waits for them, and re-layouts  7.98 us
    dot_general x2, matrix products, local(): jnp.dot(receive_table, recv_proj, preferred_element_type=jnp.float32)  6.71 us
    dot_general x2, matrix products, local(): jnp.dot(aggregated, node_in[layer_index, 1], preferred_element_type=jnp.f...  6.66 us
    convert_element_type x1, other arithmetic, local(): (edge_state.astype(jnp.float32) + message.astype(jnp.float32)).astype(jnp...  6.39 us
    reduce_sum x4, other arithmetic, layer_norm(): variance = jnp.mean(centered * centered, axis=-1, keepdims=True)  6.35 us
  transfers between devices with their start and end apart: 2, of which 2 were waited for; matrix products, arithmetic and copies ran while one was open for 16% of the time, Pallas kernels for 0%

commit v1 on v0

v1 whole, which is shorter than its diff:
```python
import jax
import jax.numpy as jnp
from jax import lax
from jax.experimental import pallas as pl
from jax.experimental.pallas import tpu as pltpu
from jax.sharding import PartitionSpec as P

MESH = pl.DeviceIdType.MESH
BF = jnp.bfloat16
F32 = jnp.float32

PEERS, CAP, NODES, EDGES, D = 128, 4, 256, 2048, 512
HALF = EDGES // 2
SLOTS = PEERS * CAP
NX, NZ, NY = 4, 8, 4
TILE = 256
DZ_ORDER = (4, 3, 5, 2, 6, 1, 7)


def dot(a, b):
    return jnp.dot(a, b, preferred_element_type=F32)


def silu(v):
    half = 0.5 * v
    return half * jnp.tanh(half) + half


def layer_norm(values, gain, shift):
    mean = jnp.mean(values, axis=-1, keepdims=True)
    centered = values - mean
    variance = jnp.mean(centered * centered, axis=-1, keepdims=True)
    return centered * lax.rsqrt(variance + 1e-05) * gain + shift


def swap_pairs(even, odd):
    low = lax.broadcasted_iota(jnp.int32, (1, 8, 128), 1) < 4
    first = jnp.where(low, even, pltpu.roll(odd, 4, 1))
    second = jnp.where(low, pltpu.roll(even, 4, 1), odd)
    return first, second


def kernel(
    node_hbm, edge_hbm, sender_hbm, receiver_hbm, mask_hbm, list_hbm,
    edge_in_hbm, edge_out_hbm, node_in_hbm, node_out_hbm, bias_hbm, gain_hbm, shift_hbm,
    node_out_ref, edge_out_ref,
    xl, xr, tr, agg_t, msg, hpre, wcat, w_send, w_recv, w_out, n_in, n_out,
    node_state, pick, sbuf, rbuf, halo, agg_acc, nh_pre, mask_col,
    sender_ref, receiver_ref, mask_ref, list_ref, bias_ref, gain_ref, shift_ref,
    ssem, rsem, ready, lsem, osem,
):
    me = lax.axis_index("dom")
    x, z, y = lax.rem(me, NX), lax.rem(me // NX, NZ), me // (NX * NZ)

    def peer(dx, dz, dy):
        return (lax.rem(y + dy, NY) * NZ + lax.rem(z + dz, NZ)) * NX + lax.rem(x + dx, NX)

    def tell(sem, target):
        pl.semaphore_signal(sem, inc=1, device_id={"dom": target}, device_id_type=MESH)

    barrier = pltpu.get_barrier_semaphore()
    for dz in range(1, NZ):
        tell(barrier, peer(0, dz, 0))
    for plane in range(1, NX * NY):
        tell(barrier, peer(plane % NX, 0, plane // NX))

    loads = {}

    def load(name, src, dst):
        copy = pltpu.make_async_copy(src, dst, lsem.at[len(loads)])
        copy.start()
        loads[name] = copy

    load("list", list_hbm, list_ref)
    load("node", node_hbm, node_state)
    load("send0", edge_in_hbm.at[0, 1], w_send.at[0])
    load("senders", sender_hbm, sender_ref)
    load("receivers", receiver_hbm, receiver_ref)
    load("masks", mask_hbm, mask_ref)
    load("biases", bias_hbm, bias_ref)
    load("gains", gain_hbm, gain_ref)
    load("shifts", shift_hbm, shift_ref)
    load("recv0", edge_in_hbm.at[0, 2], w_recv.at[0])
    load("edge0", edge_in_hbm.at[0, 0], wcat.at[0, pl.ds(0, D)])
    load("xl", edge_hbm.at[pl.ds(0, HALF)], xl.at[:, pl.ds(0, D)])
    load("out0", edge_out_hbm.at[0], w_out.at[0])
    load("xr", edge_hbm.at[pl.ds(HALF, HALF)], xr.at[:, pl.ds(0, D)])
    load("nin0", node_in_hbm.at[0], n_in.at[0])
    load("nout0", node_out_hbm.at[0], n_out.at[0])
    load("send1", edge_in_hbm.at[1, 1], w_send.at[1])
    load("recv1", edge_in_hbm.at[1, 2], w_recv.at[1])
    load("edge1", edge_in_hbm.at[1, 0], wcat.at[1, pl.ds(0, D)])
    load("out1", edge_out_hbm.at[1], w_out.at[1])
    load("nin1", node_in_hbm.at[1], n_in.at[1])
    load("nout1", node_out_hbm.at[1], n_out.at[1])

    slot_row = lax.broadcasted_iota(jnp.int32, (SLOTS, PEERS), 0)
    spread = (slot_row // CAP == lax.broadcasted_iota(jnp.int32, (SLOTS, PEERS), 1)).astype(BF)
    loads["list"].wait()
    lists = lax.dot_general(
        spread, list_ref[...].astype(F32).astype(BF), (((1,), (1,)), ((), ())), preferred_element_type=F32
    )
    own = lax.broadcasted_iota(jnp.int32, (SLOTS, CAP), 0) % CAP == lax.broadcasted_iota(
        jnp.int32, (SLOTS, CAP), 1
    )
    chosen = jnp.sum(jnp.where(own, lists, 0.0), axis=1, keepdims=True).astype(jnp.int32)
    pick[...] = (chosen == lax.broadcasted_iota(jnp.int32, (SLOTS, NODES), 1)).astype(BF)
    for r in range(2):
        rbuf[r, me] = jnp.zeros((16, 128), BF)

    def project_and_pack(r):
        loads[f"send{r}"].wait()
        send_proj = dot(node_state[...], w_send[r]).astype(BF)
        wcat[r, pl.ds(D + NODES, NODES), :] = send_proj
        rows = dot(pick[...], send_proj)
        for h in range(2):
            first, second = swap_pairs(
                rows[:, 256 * h : 256 * h + 128].reshape(PEERS // 2, 8, 128),
                rows[:, 256 * h + 128 : 256 * h + 256].reshape(PEERS // 2, 8, 128),
            )
            part = jnp.stack([first, second], axis=1).reshape(PEERS, 8, 128)
            if h == 0:
                upper = part
        sbuf[...] = jnp.concatenate([upper, part], axis=1).astype(BF)

    def send(r, target):
        pltpu.make_async_remote_copy(
            src_ref=sbuf.at[target],
            dst_ref=rbuf.at[r, me],
            send_sem=ssem.at[r],
            recv_sem=rsem.at[r],
            device_id={"dom": target},
            device_id_type=MESH,
        ).start()

    def send_far(r):
        def body(j, carry):
            plane = NX * NY - 1 - j
            for dz in DZ_ORDER:
                send(r, peer(lax.rem(plane, NX), dz, plane // NX))
            return carry

        lax.fori_loop(0, NX * NY - 1, body, 0)

    def send_line(r):
        for dz in DZ_ORDER:
            send(r, peer(0, dz, 0))

    def send_plane(r):
        def body(plane, carry):
            send(r, peer(lax.rem(plane, NX), 0, plane // NX))
            return carry

        lax.fori_loop(1, NX * NY, body, 0)

    def receive(r):
        everything = pltpu.make_async_remote_copy(
            src_ref=sbuf.at[pl.ds(0, PEERS - 1)],
            dst_ref=rbuf.at[r, pl.ds(0, PEERS - 1)],
            send_sem=ssem.at[r],
            recv_sem=rsem.at[r],
            device_id={"dom": lax.rem(me + 1, PEERS)},
            device_id_type=MESH,
        )
        everything.wait_send()
        everything.wait_recv()
        got = rbuf[r].astype(F32).reshape(PEERS // 2, 2, 2, 8, 128)
        for h in range(2):
            first, second = swap_pairs(got[:, 0, h], got[:, 1, h])
            halo[:, 256 * h : 256 * h + 128] = first.reshape(SLOTS, 128).astype(BF)
            halo[:, 256 * h + 128 : 256 * h + 256] = second.reshape(SLOTS, 128).astype(BF)

    def tables():
        senders = jnp.transpose(sender_ref[...])
        receivers = jnp.transpose(receiver_ref[...])
        masks = jnp.transpose(mask_ref[...])
        nodes = lax.broadcasted_iota(jnp.int32, (128, NODES), 1)
        slots = lax.broadcasted_iota(jnp.int32, (128, SLOTS), 1)
        node_rows = lax.broadcasted_iota(jnp.int32, (NODES, 128), 0)
        for j in range(EDGES // 128):
            rows = pl.ds(j % 8 * 128, 128)
            mask_col[pl.ds(j * 128, 128), :] = masks[:, j : j + 1].astype(F32)
            received = (receivers[:, j : j + 1] == nodes).astype(BF)
            if j < 8:
                xl[rows, pl.ds(D, NODES)] = received
                xl[rows, pl.ds(D + NODES, NODES)] = (senders[:, j : j + 1] == nodes).astype(BF)
            else:
                xr[rows, pl.ds(D, NODES)] = received
                tr[rows, :] = (senders[:, j : j + 1] - NODES == slots).astype(BF)
            live = jnp.where(mask_ref[j : j + 1, :] > 0, receiver_ref[j : j + 1, :], -1)
            agg_t[:, pl.ds(j * 128, 128)] = (live == node_rows).astype(BF)

    def edge_tail(r, hidden, state, live):
        act = silu(hidden).astype(BF)
        projected = dot(act, w_out[r]) + bias_ref[r, 1:2, :]
        message = layer_norm(projected, gain_ref[r, 0:1, :], shift_ref[r, 0:1, :]).astype(BF)
        kept = jnp.where(live > 0, message.astype(F32), 0.0)
        return message, (state.astype(F32) + kept).astype(BF)

    def local_edges(r):
        def body(t, carry):
            rows = pl.ds(pl.multiple_of(t * TILE, TILE), TILE)
            hidden = dot(xl[rows, :], wcat[r]) + bias_ref[r, 0:1, :]
            message, state = edge_tail(r, hidden, xl[rows, pl.ds(0, D)], mask_col[rows, :])
            xl[rows, pl.ds(0, D)] = state
            msg[rows, :] = message
            return carry

        lax.fori_loop(0, HALF // TILE, body, 0)
        agg_acc[...] = dot(agg_t[:, pl.ds(0, HALF)], msg[...])

    def remote_start(r):
        def body(t, carry):
            rows = pl.ds(pl.multiple_of(t * TILE, TILE), TILE)
            hpre[rows, :] = dot(xr[rows, :], wcat[r, pl.ds(0, D + NODES), :]) + bias_ref[r, 0:1, :]
            return carry

        lax.fori_loop(0, HALF // TILE, body, 0)

    def remote_edges(r):
        def body(t, carry):
            rows = pl.ds(pl.multiple_of(t * TILE, TILE), TILE)
            masks = mask_col[pl.ds(pl.multiple_of(HALF + t * TILE, TILE), TILE), :]
            hidden = dot(tr[rows, :], halo[...]) + hpre[rows, :]
            message, state = edge_tail(r, hidden, xr[rows, pl.ds(0, D)], masks)
            xr[rows, pl.ds(0, D)] = state
            msg[rows, :] = message
            return carry

        lax.fori_loop(0, HALF // TILE, body, 0)

    def write(k, src, dst):
        copy = pltpu.make_async_copy(src, dst, osem.at[k])
        copy.start()
        return copy

    loads["node"].wait()
    project_and_pack(0)
    pl.semaphore_wait(barrier, NZ - 1 + NX * NY - 1)
    for plane in range(1, NX * NY):
        tell(ready, peer(plane % NX, 0, plane // NX))
    send_line(0)
    pl.semaphore_wait(ready, NX * NY - 1)
    send_far(0)
    send_plane(0)
    for name in ("senders", "receivers", "masks", "biases", "gains", "shifts"):
        loads[name].wait()
    tables()

    writes = []
    for r in range(2):
        loads[f"recv{r}"].wait()
        wcat[r, pl.ds(D, NODES), :] = dot(node_state[...], w_recv[r]).astype(BF)
        if r == 0:
            loads["xl"].wait()
            loads["xr"].wait()
        loads[f"edge{r}"].wait()
        loads[f"out{r}"].wait()
        local_edges(r)
        if r == 1:
            writes.append(write(0, xl.at[:, pl.ds(0, D)], edge_out_ref.at[pl.ds(0, HALF)]))
        remote_start(r)
        loads[f"nin{r}"].wait()
        loads[f"nout{r}"].wait()
        nh_pre[...] = dot(node_state[...], n_in[r, 0]) + bias_ref[r, 2:3, :]
        receive(r)
        remote_edges(r)
        if r == 1:
            writes.append(write(1, xr.at[:, pl.ds(0, D)], edge_out_ref.at[pl.ds(HALF, HALF)]))
        total = (agg_acc[...] + dot(agg_t[:, pl.ds(HALF, HALF)], msg[...])).astype(BF)
        act = silu(nh_pre[...] + dot(total, n_in[r, 1])).astype(BF)
        projected = dot(act, n_out[r]) + bias_ref[r, 3:4, :]
        update = layer_norm(projected, gain_ref[r, 1:2, :], shift_ref[r, 1:2, :])
        node_state[...] = (node_state[...].astype(F32) + update).astype(BF)
        if r == 0:
            project_and_pack(1)
            send_far(1)
            send_line(1)
            send_plane(1)
    writes.append(write(2, node_state, node_out_ref))
    for copy in writes:
        copy.wait()


def local(
    node_latent, edge_latent, edge_sender, edge_receiver, edge_mask, send_list,
    edge_in, edge_out, node_in, node_out, biases, ln_gain, ln_shift,
):
    hbm = pl.BlockSpec(memory_space=pltpu.HBM)
    return pl.pallas_call(
        kernel,
        out_shape=(
            jax.ShapeDtypeStruct((NODES, D), BF),
            jax.ShapeDtypeStruct((EDGES, D), BF),
        ),
        in_specs=[hbm] * 13,
        out_specs=(hbm, hbm),
        scratch_shapes=[
            pltpu.VMEM((HALF, D + 2 * NODES), BF),
            pltpu.VMEM((HALF, D + NODES), BF),
            pltpu.VMEM((HALF, SLOTS), BF),
            pltpu.VMEM((NODES, EDGES), BF),
            pltpu.VMEM((HALF, D), BF),
            pltpu.VMEM((HALF, D), F32),
            pltpu.VMEM((2, D + 2 * NODES, D), BF),
            pltpu.VMEM((2, D, D), BF),
            pltpu.VMEM((2, D, D), BF),
            pltpu.VMEM((2, D, D), BF),
            pltpu.VMEM((2, 2, D, D), BF),
            pltpu.VMEM((2, D, D), BF),
            pltpu.VMEM((NODES, D), BF),
            pltpu.VMEM((SLOTS, NODES), BF),
            pltpu.VMEM((PEERS, 16, 128), BF),
            pltpu.VMEM((2, PEERS, 16, 128), BF),
            pltpu.VMEM((SLOTS, D), BF),
            pltpu.VMEM((NODES, D), F32),
            pltpu.VMEM((NODES, D), F32),
            pltpu.VMEM((EDGES, 1), F32),
            pltpu.VMEM((16, 128), jnp.int32),
            pltpu.VMEM((16, 128), jnp.int32),
            pltpu.VMEM((16, 128), jnp.int32),
            pltpu.VMEM((CAP, PEERS), jnp.int32),
            pltpu.VMEM((2, 4, D), F32),
            pltpu.VMEM((2, 2, D), F32),
            pltpu.VMEM((2, 2, D), F32),
            pltpu.SemaphoreType.DMA((2,)),
            pltpu.SemaphoreType.DMA((2,)),
            pltpu.SemaphoreType.REGULAR,
            pltpu.SemaphoreType.DMA((22,)),
            pltpu.SemaphoreType.DMA((3,)),
        ],
        compiler_params=pltpu.CompilerParams(
            collective_id=0, has_side_effects=True, vmem_limit_bytes=52 * 2**20
        ),
    )(
        node_latent, edge_latent,
        edge_sender.reshape(16, 128), edge_receiver.reshape(16, 128), edge_mask.reshape(16, 128),
        send_list.reshape(PEERS, CAP).T,
        edge_in, edge_out, node_in, node_out, biases, ln_gain, ln_shift,
    )


def solution(mesh):
    in_specs = (
        P(("dp", "dom"), None),
        P(("dp", "dom"), None),
        P(("dp", "dom")),
        P(("dp", "dom")),
        P(("dp", "dom")),
        P(("dp", "dom"), None, None),
        P(),
        P(),
        P(),
        P(),
        P(),
        P(),
        P(),
    )
    out_specs = (P(("dp", "dom"), None), P(("dp", "dom"), None))
    return jax.shard_map(local, mesh=mesh, in_specs=in_specs, out_specs=out_specs, check_vma=False)
```

time: 125 us -> 61.5 us (0.49)
  Pallas kernels: 0 us -> 49.5 us
  matrix products: 49.4 us -> 0 us
  starting transfers between devices: 23 us -> 0 us
  other arithmetic: 18.6 us -> 0 us
  waiting for transfers between devices: 16.7 us -> 0 us
  local copies, waits for them, and re-layouts: 15.5 us -> 10.8 us
    pallas_call x0 -> x1, Pallas kernels: none -> 49.5 us  [local(): pl.pallas_call(kernel, out_shape=(jax.ShapeDtypeStruct((NODES, D), BF), j...]
    dot_general x16 -> x0, matrix products: 49.4 us -> none  [the longest x2 16 us: edge_message(): jnp.dot(activated, w_output, preferred_element_type=jnp.float32)]
    all_to_all x2 -> x0, starting transfers between devices: 23 us -> none  [local(): lax.all_to_all(outgoing, 'dom', split_axis=0, concat_axis=0, tiled=True)]
    all_to_all x2 -> x0, waiting for transfers between devices: 16.7 us -> none  [local(): lax.all_to_all(outgoing, 'dom', split_axis=0, concat_axis=0, tiled=True)]
    convert_element_type x3 -> x0, other arithmetic: 7.48 us -> none  [the longest x1 6.39 us: local(): (edge_state.astype(jnp.float32) + message.astype(jnp.float32)).astype(jnp...]
    reduce_sum x4 -> x0, other arithmetic: 6.35 us -> none  [layer_norm(): variance = jnp.mean(centered * centered, axis=-1, keepdims=True)]
    gather x4 -> x0, local copies, waits for them, and re-layouts: 5.25 us -> none  [local(): outgoing = jnp.where(present[:, :, None], node_state[pick_rows], zero_bf)]
    select_n x3 -> x0, other arithmetic: 3.34 us -> none  [the longest x2 2.3 us: local(): outgoing = jnp.where(present[:, :, None], node_state[pick_rows], zero_bf)]
  transfers between devices with their start and end apart: 2 -> 0, of which waited for: 2 -> 0; matrix products, arithmetic and copies ran while one was open for 16% -> 0% of each run, Pallas kernels for 0% -> 0%
where the time goes in v1:
time: 61.5 us; the launch traced here: 60.9 us
  Pallas kernels  49.5 us (80%)
  local copies, waits for them, and re-layouts  10.8 us (18%)
  between operations  0.66 us (1%)
    pallas_call x1, Pallas kernels, local(): pl.pallas_call(kernel, out_shape=(jax.ShapeDtypeStruct((NODES, D), BF), j...  49.5 us
    unnamed x20, local copies, waits for them, and re-layouts  10.8 us

profile of v1, /device:TPU:2, one launch (start us, length us, event | category | flops | bytes accessed | tf_op | source)
XLA Modules:
  0.0 60.9 jit_solution(307519218663610321)
XLA Ops:
  0.6 0.0 copy-start
  0.6 1.2 %copy-done = bf16[2,512,512]{2,1,0:T(8,128)(2,1)S(1)} copy-done((bf16[2,512,512]{2,1,0:T(8,128)(2,1)S(1)}, bf16[2,512,512]{2,1,0:T(8,128)(2,1)}, u32[]{:S(2)}) %copy-start) | copy-done | bytes 1048600
  1.9 0.0 copy-start.1
  1.9 0.9 %copy-done.1 = bf16[256,512]{1,0:T(8,128)(2,1)S(1)} copy-done((bf16[256,512]{1,0:T(8,128)(2,1)S(1)}, bf16[256,512]{1,0:T(8,128)(2,1)}, u32[]{:S(2)}) %copy-start.1) | copy-done | bytes 262168
  2.8 0.0 copy-start.2
  2.8 0.7 %copy-done.2 = f32[2,4,512]{2,1,0:T(4,128)S(1)} copy-done((f32[2,4,512]{2,1,0:T(4,128)S(1)}, f32[2,4,512]{2,1,0:T(4,128)}, u32[]{:S(2)}) %copy-start.2) | copy-done | bytes 16408
  3.5 0.0 copy-start.3
  3.5 0.7 %copy-done.3 = s32[2048]{0:T(1024)S(1)} copy-done((s32[2048]{0:T(1024)S(1)}, s32[2048]{0:T(1024)}, u32[]{:S(2)}) %copy-start.3) | copy-done | bytes 8216
  4.2 0.0 copy-start.4
  4.2 0.7 %copy-done.4 = s32[2048]{0:T(1024)S(1)} copy-done((s32[2048]{0:T(1024)S(1)}, s32[2048]{0:T(1024)}, u32[]{:S(2)}) %copy-start.4) | copy-done | bytes 8216
  4.9 0.0 copy-start.5
  4.9 0.7 %copy-done.5 = s32[2048]{0:T(1024)S(1)} copy-done((s32[2048]{0:T(1024)S(1)}, s32[2048]{0:T(1024)}, u32[]{:S(2)}) %copy-start.5) | copy-done | bytes 8216
  5.6 0.0 copy-start.6
  5.6 0.7 %copy-done.6 = f32[2,2,512]{2,1,0:T(2,128)S(1)} copy-done((f32[2,2,512]{2,1,0:T(2,128)S(1)}, f32[2,2,512]{2,1,0:T(2,128)}, u32[]{:S(2)}) %copy-start.6) | copy-done | bytes 8216
  6.3 0.0 copy-start.7
  6.3 0.7 %copy-done.7 = f32[2,2,512]{2,1,0:T(2,128)S(1)} copy-done((f32[2,2,512]{2,1,0:T(2,128)S(1)}, f32[2,2,512]{2,1,0:T(2,128)}, u32[]{:S(2)}) %copy-start.7) | copy-done | bytes 8216
  7.0 0.0 copy-start.8
  7.0 0.7 %copy-done.8 = s32[1,128,4]{1,2,0:T(4,128)S(1)} copy-done((s32[1,128,4]{1,2,0:T(4,128)S(1)}, s32[1,128,4]{1,2,0:T(4,128)}, u32[]{:S(2)}) %copy-start.8) | copy-done | bytes 2072
  7.7 49.5 %shard_map.140 = (bf16[256,512]{1,0:T(8,128)(2,1)S(1)}, bf16[2048,512]{1,0:T(8,128)(2,1)}) custom-call(bf16[256,512]{1,0:T(8,128)(2,1)S(1)} %copy-done.1, bf16[2048,512]{1,0:T(8,128)(2,1)} %edge_hbm.1, s32[16,128]{1,0:T(8,128)S(1)} %bitcast.6, s32[16,128]{1,0:T(8,128)S(1)} %bitcast.7, s32[16,128]{1,0:T(8,128)S(1)} %bitcast.8, s32[4,128]{1,0:T(4,128)S(1)} %bitcast.9, ...), custom_call_target="tpu_custom_call" | custom-call | tf_op jit(solution)/shard_map/pallas_call | solution.py:290
  57.2 0.7 %copy.17 = bf16[256,512]{1,0:T(8,128)(2,1)} copy(bf16[256,512]{1,0:T(8,128)(2,1)S(1)} %get-tuple-element.4) | data formatting | bytes 524288
  57.9 3.0 %copy.18 = bf16[2048,512]{1,0:T(8,128)(2,1)} copy(bf16[2048,512]{1,0:T(8,128)(2,1)} %get-tuple-element.5) | data formatting | bytes 4194304
Async XLA Ops:
  0.6 1.2 %copy-start = (bf16[2,512,512]{2,1,0:T(8,128)(2,1)S(1)}, bf16[2,512,512]{2,1,0:T(8,128)(2,1)}, u32[]{:S(2)}) copy-start(bf16[2,512,512]{2,1,0:T(8,128)(2,1)} %edge_out_hbm.1) | copy-start | bytes 3145732
  1.9 0.9 %copy-start.1 = (bf16[256,512]{1,0:T(8,128)(2,1)S(1)}, bf16[256,512]{1,0:T(8,128)(2,1)}, u32[]{:S(2)}) copy-start(bf16[256,512]{1,0:T(8,128)(2,1)} %node_hbm.1) | copy-start | bytes 786436
  2.8 0.7 %copy-start.2 = (f32[2,4,512]{2,1,0:T(4,128)S(1)}, f32[2,4,512]{2,1,0:T(4,128)}, u32[]{:S(2)}) copy-start(f32[2,4,512]{2,1,0:T(4,128)} %bias_hbm.1) | copy-start | bytes 49156
  3.5 0.7 %copy-start.3 = (s32[2048]{0:T(1024)S(1)}, s32[2048]{0:T(1024)}, u32[]{:S(2)}) copy-start(s32[2048]{0:T(1024)} %param.15) | copy-start | bytes 24580
  4.2 0.7 %copy-start.4 = (s32[2048]{0:T(1024)S(1)}, s32[2048]{0:T(1024)}, u32[]{:S(2)}) copy-start(s32[2048]{0:T(1024)} %param.16) | copy-start | bytes 24580
  4.9 0.7 %copy-start.5 = (s32[2048]{0:T(1024)S(1)}, s32[2048]{0:T(1024)}, u32[]{:S(2)}) copy-start(s32[2048]{0:T(1024)} %param.17) | copy-start | bytes 24580
  5.6 0.7 %copy-start.6 = (f32[2,2,512]{2,1,0:T(2,128)S(1)}, f32[2,2,512]{2,1,0:T(2,128)}, u32[]{:S(2)}) copy-start(f32[2,2,512]{2,1,0:T(2,128)} %gain_hbm.1) | copy-start | bytes 24580
  6.3 0.7 %copy-start.7 = (f32[2,2,512]{2,1,0:T(2,128)S(1)}, f32[2,2,512]{2,1,0:T(2,128)}, u32[]{:S(2)}) copy-start(f32[2,2,512]{2,1,0:T(2,128)} %shift_hbm.1) | copy-start | bytes 24580
  7.0 0.7 %copy-start.8 = (s32[1,128,4]{1,2,0:T(4,128)S(1)}, s32[1,128,4]{1,2,0:T(4,128)}, u32[]{:S(2)}) copy-start(s32[1,128,4]{1,2,0:T(4,128)} %param.18) | copy-start | bytes 6148

commit v2 on v1

--- a/solution.py
+++ b/solution.py
@@ -40,14 +40,43 @@
     return first, second
 
 
+def edge_tail(hidden, state, live, w_out, bias, gain, shift):
+    act = silu(hidden).astype(BF)
+    projected = dot(act, w_out) + bias[1:2, :]
+    message = layer_norm(projected, gain[0:1, :], shift[0:1, :]).astype(BF)
+    kept = jnp.where(live > 0, message.astype(F32), 0.0)
+    return message, (state.astype(F32) + kept).astype(BF)
+
+
+def remote_edges(tr, halo, hpre, xr, mask_col, msg, state_ref, w_out, bias, gain, shift):
+    def body(t, carry):
+        rows = pl.ds(pl.multiple_of(t * TILE, TILE), TILE)
+        masks = mask_col[pl.ds(pl.multiple_of(HALF + t * TILE, TILE), TILE), :]
+        hidden = dot(tr[rows, :], halo[...]) + hpre[rows, :]
+        message, state = edge_tail(hidden, xr[rows, pl.ds(0, D)], masks, w_out, bias, gain, shift)
+        state_ref[rows, pl.ds(0, D)] = state
+        msg[rows, :] = message
+        return carry
+
+    lax.fori_loop(0, HALF // TILE, body, 0)
+
+
+def node_step(agg_acc, agg_t, msg, nh_pre, node_state, w_in, w_out, bias, gain, shift):
+    total = (agg_acc[...] + dot(agg_t[:, pl.ds(HALF, HALF)], msg[...])).astype(BF)
+    act = silu(nh_pre[...] + dot(total, w_in)).astype(BF)
+    projected = dot(act, w_out) + bias[3:4, :]
+    update = layer_norm(projected, gain[1:2, :], shift[1:2, :])
+    return (node_state[...].astype(F32) + update).astype(BF)
+
+
 def kernel(
     node_hbm, edge_hbm, sender_hbm, receiver_hbm, mask_hbm, list_hbm,
     edge_in_hbm, edge_out_hbm, node_in_hbm, node_out_hbm, bias_hbm, gain_hbm, shift_hbm,
-    node_out_ref, edge_out_ref,
-    xl, xr, tr, agg_t, msg, hpre, wcat, w_send, w_recv, w_out, n_in, n_out,
-    node_state, pick, sbuf, rbuf, halo, agg_acc, nh_pre, mask_col,
-    sender_ref, receiver_ref, mask_ref, list_ref, bias_ref, gain_ref, shift_ref,
-    ssem, rsem, ready, lsem, osem,
+    xl, xr, tr, agg_t, hpre, halo, agg_acc, nh_pre, node_state, mask_col,
+    w_out, n_in, n_out, bias_ref, gain_ref, shift_ref,
+    msg, wcat, w_send, w_recv, pick, sbuf, rbuf,
+    sender_ref, receiver_ref, mask_ref, list_ref,
+    ssem, rsem, ready, lsem,
 ):
     me = lax.axis_index("dom")
     x, z, y = lax.rem(me, NX), lax.rem(me // NX, NZ), me // (NX * NZ)
@@ -190,18 +219,14 @@
             live = jnp.where(mask_ref[j : j + 1, :] > 0, receiver_ref[j : j + 1, :], -1)
             agg_t[:, pl.ds(j * 128, 128)] = (live == node_rows).astype(BF)
 
-    def edge_tail(r, hidden, state, live):
-        act = silu(hidden).astype(BF)
-        projected = dot(act, w_out[r]) + bias_ref[r, 1:2, :]
-        message = layer_norm(projected, gain_ref[r, 0:1, :], shift_ref[r, 0:1, :]).astype(BF)
-        kept = jnp.where(live > 0, message.astype(F32), 0.0)
-        return message, (state.astype(F32) + kept).astype(BF)
-
     def local_edges(r):
         def body(t, carry):
             rows = pl.ds(pl.multiple_of(t * TILE, TILE), TILE)
             hidden = dot(xl[rows, :], wcat[r]) + bias_ref[r, 0:1, :]
-            message, state = edge_tail(r, hidden, xl[rows, pl.ds(0, D)], mask_col[rows, :])
+            message, state = edge_tail(
+                hidden, xl[rows, pl.ds(0, D)], mask_col[rows, :],
+                w_out[r], bias_ref[r], gain_ref[r], shift_ref[r],
+            )
             xl[rows, pl.ds(0, D)] = state
             msg[rows, :] = message
             return carry
@@ -216,23 +241,6 @@
             return carry
 
         lax.fori_loop(0, HALF // TILE, body, 0)
-
-    def remote_edges(r):
-        def body(t, carry):
-            rows = pl.ds(pl.multiple_of(t * TILE, TILE), TILE)
-            masks = mask_col[pl.ds(pl.multiple_of(HALF + t * TILE, TILE), TILE), :]
-            hidden = dot(tr[rows, :], halo[...]) + hpre[rows, :]
-            message, state = edge_tail(r, hidden, xr[rows, pl.ds(0, D)], masks)
-            xr[rows, pl.ds(0, D)] = state
-            msg[rows, :] = message
-            return carry
-
-        lax.fori_loop(0, HALF // TILE, body, 0)
-
-    def write(k, src, dst):
-        copy = pltpu.make_async_copy(src, dst, osem.at[k])
-        copy.start()
-        return copy
 
     loads["node"].wait()
     project_and_pack(0)
@@ -247,7 +255,6 @@
         loads[name].wait()
     tables()
 
-    writes = []
     for r in range(2):
         loads[f"recv{r}"].wait()
         wcat[r, pl.ds(D, NODES), :] = dot(node_state[...], w_recv[r]).astype(BF)
@@ -257,29 +264,49 @@
         loads[f"edge{r}"].wait()
         loads[f"out{r}"].wait()
         local_edges(r)
-        if r == 1:
-            writes.append(write(0, xl.at[:, pl.ds(0, D)], edge_out_ref.at[pl.ds(0, HALF)]))
         remote_start(r)
         loads[f"nin{r}"].wait()
         loads[f"nout{r}"].wait()
         nh_pre[...] = dot(node_state[...], n_in[r, 0]) + bias_ref[r, 2:3, :]
         receive(r)
-        remote_edges(r)
-        if r == 1:
-            writes.append(write(1, xr.at[:, pl.ds(0, D)], edge_out_ref.at[pl.ds(HALF, HALF)]))
-        total = (agg_acc[...] + dot(agg_t[:, pl.ds(HALF, HALF)], msg[...])).astype(BF)
-        act = silu(nh_pre[...] + dot(total, n_in[r, 1])).astype(BF)
-        projected = dot(act, n_out[r]) + bias_ref[r, 3:4, :]
-        update = layer_norm(projected, gain_ref[r, 1:2, :], shift_ref[r, 1:2, :])
-        node_state[...] = (node_state[...].astype(F32) + update).astype(BF)
         if r == 0:
+            remote_edges(
+                tr, halo, hpre, xr, mask_col, msg, xr,
+                w_out[r], bias_ref[r], gain_ref[r], shift_ref[r],
+            )
+            node_state[...] = node_step(
+                agg_acc, agg_t, msg, nh_pre, node_state,
+                n_in[r, 1], n_out[r], bias_ref[r], gain_ref[r], shift_ref[r],
+            )
             project_and_pack(1)
             send_far(1)
             send_line(1)
             send_plane(1)
-    writes.append(write(2, node_state, node_out_ref))
-    for copy in writes:
-        copy.wait()
+
+
+def finish(
+    xl, xr, tr, agg_t, hpre, halo, agg_acc, nh_pre, node_state, mask_col,
+    w_out, n_in, n_out, bias_ref, gain_ref, shift_ref,
+    node_out_hbm, edge_out_hbm,
+    msg, state, node_new, osem,
+):
+    near = pltpu.make_async_copy(xl.at[:, pl.ds(0, D)], edge_out_hbm.at[pl.ds(0, HALF)], osem.at[0])
+    near.start()
+    remote_edges(
+        tr, halo, hpre, xr, mask_col, msg, state,
+        w_out[1], bias_ref[1], gain_ref[1], shift_ref[1],
+    )
+    far = pltpu.make_async_copy(state, edge_out_hbm.at[pl.ds(HALF, HALF)], osem.at[1])
+    far.start()
+    node_new[...] = node_step(
+        agg_acc, agg_t, msg, nh_pre, node_state,
+        n_in[1, 1], n_out[1], bias_ref[1], gain_ref[1], shift_ref[1],
+    )
+    nodes = pltpu.make_async_copy(node_new, node_out_hbm, osem.at[2])
+    nodes.start()
+    near.wait()
+    far.wait()
+    nodes.wait()
 
 
 def local(
@@ -287,57 +314,70 @@
     edge_in, edge_out, node_in, node_out, biases, ln_gain, ln_shift,
 ):
     hbm = pl.BlockSpec(memory_space=pltpu.HBM)
-    return pl.pallas_call(
+    vmem = pl.BlockSpec(memory_space=pltpu.VMEM)
+    args = [
+        node_latent, edge_latent,
+        edge_sender.reshape(16, 128), edge_receiver.reshape(16, 128), edge_mask.reshape(16, 128),
+        send_list.reshape(PEERS, CAP).T,
+        edge_in, edge_out, node_in, node_out, biases, ln_gain, ln_shift,
+    ]
+    held = (
+        pltpu.VMEM((HALF, D + 2 * NODES), BF),
+        pltpu.VMEM((HALF, D + NODES), BF),
+        pltpu.VMEM((HALF, SLOTS), BF),
+        pltpu.VMEM((NODES, EDGES), BF),
+        pltpu.VMEM((HALF, D), F32),
+        pltpu.VMEM((SLOTS, D), BF),
+        pltpu.VMEM((NODES, D), F32),
+        pltpu.VMEM((NODES, D), F32),
+        pltpu.VMEM((NODES, D), BF),
+        pltpu.VMEM((EDGES, 1), F32),
+        pltpu.VMEM((2, D, D), BF),
+        pltpu.VMEM((2, 2, D, D), BF),
+        pltpu.VMEM((2, D, D), BF),
+        pltpu.VMEM((2, 4, D), F32),
+        pltpu.VMEM((2, 2, D), F32),
+        pltpu.VMEM((2, 2, D), F32),
+    )
+    passed = pl.pallas_call(
         kernel,
-        out_shape=(
-            jax.ShapeDtypeStruct((NODES, D), BF),
-            jax.ShapeDtypeStruct((EDGES, D), BF),
-        ),
+        out_shape=held,
         in_specs=[hbm] * 13,
-        out_specs=(hbm, hbm),
+        out_specs=(vmem,) * len(held),
         scratch_shapes=[
-            pltpu.VMEM((HALF, D + 2 * NODES), BF),
-            pltpu.VMEM((HALF, D + NODES), BF),
-            pltpu.VMEM((HALF, SLOTS), BF),
-            pltpu.VMEM((NODES, EDGES), BF),
             pltpu.VMEM((HALF, D), BF),
-            pltpu.VMEM((HALF, D), F32),
             pltpu.VMEM((2, D + 2 * NODES, D), BF),
             pltpu.VMEM((2, D, D), BF),
             pltpu.VMEM((2, D, D), BF),
-            pltpu.VMEM((2, D, D), BF),
-            pltpu.VMEM((2, 2, D, D), BF),
-            pltpu.VMEM((2, D, D), BF),
-            pltpu.VMEM((NODES, D), BF),
             pltpu.VMEM((SLOTS, NODES), BF),
             pltpu.VMEM((PEERS, 16, 128), BF),
             pltpu.VMEM((2, PEERS, 16, 128), BF),
-            pltpu.VMEM((SLOTS, D), BF),
-            pltpu.VMEM((NODES, D), F32),
-            pltpu.VMEM((NODES, D), F32),
-            pltpu.VMEM((EDGES, 1), F32),
             pltpu.VMEM((16, 128), jnp.int32),
             pltpu.VMEM((16, 128), jnp.int32),
             pltpu.VMEM((16, 128), jnp.int32),
             pltpu.VMEM((CAP, PEERS), jnp.int32),
-            pltpu.VMEM((2, 4, D), F32),
-            pltpu.VMEM((2, 2, D), F32),
-            pltpu.VMEM((2, 2, D), F32),
             pltpu.SemaphoreType.DMA((2,)),
             pltpu.SemaphoreType.DMA((2,)),
             pltpu.SemaphoreType.REGULAR,
             pltpu.SemaphoreType.DMA((22,)),
+        ],
+        compiler_params=pltpu.CompilerParams(
+            collective_id=0, has_side_effects=True, vmem_limit_bytes=28 * 2**20
+        ),
+    )(*[pltpu.with_memory_space_constraint(a, pltpu.HBM) for a in args])
+    return pl.pallas_call(
+        finish,
+        out_shape=(pltpu.HBM((NODES, D), BF), pltpu.HBM((EDGES, D), BF)),
+        in_specs=[vmem] * len(held),
+        out_specs=(hbm, hbm),
+        scratch_shapes=[
+            pltpu.VMEM((HALF, D), BF),
+            pltpu.VMEM((HALF, D), BF),
+            pltpu.VMEM((NODES, D), BF),
             pltpu.SemaphoreType.DMA((3,)),
         ],
-        compiler_params=pltpu.CompilerParams(
-            collective_id=0, has_side_effects=True, vmem_limit_bytes=52 * 2**20
-        ),
-    )(
-        node_latent, edge_latent,
-        edge_sender.reshape(16, 128), edge_receiver.reshape(16, 128), edge_mask.reshape(16, 128),
-        send_list.reshape(PEERS, CAP).T,
-        edge_in, edge_out, node_in, node_out, biases, ln_gain, ln_shift,
-    )
+        compiler_params=pltpu.CompilerParams(vmem_limit_bytes=20 * 2**20),
+    )(*passed)
 
 
 def solution(mesh):

time: 61.5 us -> 51 us (0.83)
  local copies, waits for them, and re-layouts: 10.8 us -> 0 us
    unnamed x20 -> x0, local copies, waits for them, and re-layouts: 10.8 us -> none
    pallas_call x1 -> x2, Pallas kernels: 49.5 us -> 50.1 us  [the longest x1 44.8 us: local(): pl.pallas_call(kernel, out_shape=held, in_specs=[hbm] * 13, out_specs=(vm...]
where the time goes in v2:
time: 51 us; the launch traced here: 50.7 us
  Pallas kernels  50.1 us (98%)
  between operations  0.64 us (1%)
    pallas_call x1, Pallas kernels, local(): pl.pallas_call(kernel, out_shape=held, in_specs=[hbm] * 13, out_specs=(vm...  44.8 us
    pallas_call x1, Pallas kernels, local(): pl.pallas_call(finish, out_shape=(pltpu.HBM((NODES, D), BF), pltpu.HBM((E...  5.31 us

profile of v2, /device:TPU:2, one launch (start us, length us, event | category | flops | bytes accessed | tf_op | source)
XLA Modules:
  0.0 50.7 jit_solution(14017605744610632162)
XLA Ops:
  0.6 44.8 %shard_map.140 = (bf16[1024,1024]{1,0:T(8,128)(2,1)S(1)}, bf16[1024,768]{1,0:T(8,128)(2,1)S(1)}, bf16[1024,512]{1,0:T(8,128)(2,1)S(1)}, bf16[256,2048]{1,0:T(8,1...) custom-call(bf16[256,512]{1,0:T(8,128)(2,1)} %node_hbm.1, ...), custom_call_target="tpu_custom_call" | custom-call | tf_op jit(solution)/shard_map/pallas_call | solution.py:342
  45.4 5.3 %shard_map.141 = (bf16[256,512]{1,0:T(8,128)(2,1)}, bf16[2048,512]{1,0:T(8,128)(2,1)}) custom-call(bf16[1024,1024]{1,0:T(8,128)(2,1)S(1)} %get-tuple-element.18.xl, bf16[1024,768]{1,0:T(8,128)(2,1)S(1)} %get-tuple-element.19.xr, bf16[1024,512]{1,0:T(8,128)(2,1)S(1)} %get-tuple-element.20.tr, bf16[256,2048]{1,0:T(8,128)(2,1)S(1)} %get-tuple-element.21.agg_t, ...), custom_call_target="tpu_custom_call" | custom-call | tf_op jit(solution)/shard_map/pallas_call | solution.py:368

commit v3 on v2

--- a/solution.py
+++ b/solution.py
@@ -13,7 +13,7 @@
 HALF = EDGES // 2
 SLOTS = PEERS * CAP
 NX, NZ, NY = 4, 8, 4
-TILE = 256
+TILE = 512
 DZ_ORDER = (4, 3, 5, 2, 6, 1, 7)
 
 
@@ -43,9 +43,9 @@
 def edge_tail(hidden, state, live, w_out, bias, gain, shift):
     act = silu(hidden).astype(BF)
     projected = dot(act, w_out) + bias[1:2, :]
-    message = layer_norm(projected, gain[0:1, :], shift[0:1, :]).astype(BF)
-    kept = jnp.where(live > 0, message.astype(F32), 0.0)
-    return message, (state.astype(F32) + kept).astype(BF)
+    message = layer_norm(projected, gain[0:1, :], shift[0:1, :])
+    message = jnp.where(live > 0, message, 0.0).astype(BF)
+    return message, state + message
 
 
 def remote_edges(tr, halo, hpre, xr, mask_col, msg, state_ref, w_out, bias, gain, shift):
@@ -58,7 +58,7 @@
         msg[rows, :] = message
         return carry
 
-    lax.fori_loop(0, HALF // TILE, body, 0)
+    lax.fori_loop(0, HALF // TILE, body, 0, unroll=True)
 
 
 def node_step(agg_acc, agg_t, msg, nh_pre, node_state, w_in, w_out, bias, gain, shift):
@@ -87,12 +87,6 @@
     def tell(sem, target):
         pl.semaphore_signal(sem, inc=1, device_id={"dom": target}, device_id_type=MESH)
 
-    barrier = pltpu.get_barrier_semaphore()
-    for dz in range(1, NZ):
-        tell(barrier, peer(0, dz, 0))
-    for plane in range(1, NX * NY):
-        tell(barrier, peer(plane % NX, 0, plane // NX))
-
     loads = {}
 
     def load(name, src, dst):
@@ -103,6 +97,138 @@
     load("list", list_hbm, list_ref)
     load("node", node_hbm, node_state)
     load("send0", edge_in_hbm.at[0, 1], w_send.at[0])
+
+    barrier = pltpu.get_barrier_semaphore()
+    for plane in range(1, NX * NY):
+        tell(barrier, peer(plane % NX, 0, plane // NX))
+    for dz in range(1, NZ):
+        tell(barrier, peer(0, dz, 0))
+
+    slot_row = lax.broadcasted_iota(jnp.int32, (SLOTS, PEERS), 0)
+    spread = (slot_row // CAP == lax.broadcasted_iota(jnp.int32, (SLOTS, PEERS), 1)).astype(BF)
+    loads["list"].wait()
+    lists = lax.dot_general(
+        spread, list_ref[...].astype(F32).astype(BF), (((1,), (1,)), ((), ())), preferred_element_type=F32
+    )
+    own = lax.broadcasted_iota(jnp.int32, (SLOTS, CAP), 0) % CAP == lax.broadcasted_iota(
+        jnp.int32, (SLOTS, CAP), 1
+    )
+    chosen = jnp.sum(jnp.where(own, lists, 0.0), axis=1, keepdims=True).astype(jnp.int32)
+    pick[...] = (chosen == lax.broadcasted_iota(jnp.int32, (SLOTS, NODES), 1)).astype(BF)
+    for r in range(2):
+        rbuf[r, me] = jnp.zeros((16, 128), BF)
+
+    def project_and_pack(r):
+        loads[f"send{r}"].wait()
+        send_proj = dot(node_state[...], w_send[r]).astype(BF)
+        wcat[r, pl.ds(D + NODES, NODES), :] = send_proj
+        rows = dot(pick[...], send_proj)
+        for h in range(2):
+            first, second = swap_pairs(
+                rows[:, 256 * h : 256 * h + 128].reshape(PEERS // 2, 8, 128),
+                rows[:, 256 * h + 128 : 256 * h + 256].reshape(PEERS // 2, 8, 128),
+            )
+            part = jnp.stack([first, second], axis=1).reshape(PEERS, 8, 128)
+            if h == 0:
+                upper = part
+        sbuf[...] = jnp.concatenate([upper, part], axis=1).astype(BF)
+
+    def send(r, target):
+        pltpu.make_async_remote_copy(
+            src_ref=sbuf.at[target],
+            dst_ref=rbuf.at[r, me],
+            send_sem=ssem.at[r],
+            recv_sem=rsem.at[r],
+            device_id={"dom": target},
+            device_id_type=MESH,
+        ).start()
+
+    def send_far(r):
+        def body(j, carry):
+            plane = NX * NY - 1 - j
+            for dz in DZ_ORDER:
+                send(r, peer(lax.rem(plane, NX), dz, plane // NX))
+            return carry
+
+        lax.fori_loop(0, NX * NY - 1, body, 0)
+
+    def send_line(r):
+        for dz in DZ_ORDER:
+            send(r, peer(0, dz, 0))
+
+    def send_plane(r):
+        def body(plane, carry):
+            send(r, peer(lax.rem(plane, NX), 0, plane // NX))
+            return carry
+
+        lax.fori_loop(1, NX * NY, body, 0)
+
+    def receive(r):
+        everything = pltpu.make_async_remote_copy(
+            src_ref=sbuf.at[pl.ds(0, PEERS - 1)],
+            dst_ref=rbuf.at[r, pl.ds(0, PEERS - 1)],
+            send_sem=ssem.at[r],
+            recv_sem=rsem.at[r],
+            device_id={"dom": lax.rem(me + 1, PEERS)},
+            device_id_type=MESH,
+        )
+        everything.wait_send()
+        everything.wait_recv()
+        got = rbuf[r].astype(F32).reshape(PEERS // 2, 2, 2, 8, 128)
+        for h in range(2):
+            first, second = swap_pairs(got[:, 0, h], got[:, 1, h])
+            halo[:, 256 * h : 256 * h + 128] = first.reshape(SLOTS, 128).astype(BF)
+            halo[:, 256 * h + 128 : 256 * h + 256] = second.reshape(SLOTS, 128).astype(BF)
+
+    def tables():
+        senders = jnp.transpose(sender_ref[...])
+        receivers = jnp.transpose(receiver_ref[...])
+        masks = jnp.transpose(mask_ref[...])
+        nodes = lax.broadcasted_iota(jnp.int32, (128, NODES), 1)
+        slots = lax.broadcasted_iota(jnp.int32, (128, SLOTS), 1)
+        node_rows = lax.broadcasted_iota(jnp.int32, (NODES, 128), 0)
+        for j in range(EDGES // 128):
+            rows = pl.ds(j % 8 * 128, 128)
+            mask_col[pl.ds(j * 128, 128), :] = masks[:, j : j + 1].astype(F32)
+            received = (receivers[:, j : j + 1] == nodes).astype(BF)
+            if j < 8:
+                xl[rows, pl.ds(D, NODES)] = received
+                xl[rows, pl.ds(D + NODES, NODES)] = (senders[:, j : j + 1] == nodes).astype(BF)
+            else:
+                xr[rows, pl.ds(D, NODES)] = received
+                tr[rows, :] = (senders[:, j : j + 1] - NODES == slots).astype(BF)
+            live = jnp.where(mask_ref[j : j + 1, :] > 0, receiver_ref[j : j + 1, :], -1)
+            agg_t[:, pl.ds(j * 128, 128)] = (live == node_rows).astype(BF)
+
+    def local_edges(r):
+        def body(t, carry):
+            rows = pl.ds(pl.multiple_of(t * TILE, TILE), TILE)
+            hidden = dot(xl[rows, :], wcat[r]) + bias_ref[r, 0:1, :]
+            message, state = edge_tail(
+                hidden, xl[rows, pl.ds(0, D)], mask_col[rows, :],
+                w_out[r], bias_ref[r], gain_ref[r], shift_ref[r],
+            )
+            xl[rows, pl.ds(0, D)] = state
+            msg[rows, :] = message
+            return carry
+
+        lax.fori_loop(0, HALF // TILE, body, 0, unroll=True)
+        agg_acc[...] = dot(agg_t[:, pl.ds(0, HALF)], msg[...])
+
+    def remote_start(r):
+        def body(t, carry):
+            rows = pl.ds(pl.multiple_of(t * TILE, TILE), TILE)
+            hpre[rows, :] = dot(xr[rows, :], wcat[r, pl.ds(0, D + NODES), :]) + bias_ref[r, 0:1, :]
+            return carry
+
+        lax.fori_loop(0, HALF // TILE, body, 0, unroll=True)
+
+    loads["node"].wait()
+    project_and_pack(0)
+    pl.semaphore_wait(barrier, NZ - 1 + NX * NY - 1)
+    for dz in range(1, NZ):
+        tell(ready, peer(0, dz, 0))
+    send_line(0)
     load("senders", sender_hbm, sender_ref)
     load("receivers", receiver_hbm, receiver_ref)
     load("masks", mask_hbm, mask_ref)
@@ -122,133 +248,7 @@
     load("out1", edge_out_hbm.at[1], w_out.at[1])
     load("nin1", node_in_hbm.at[1], n_in.at[1])
     load("nout1", node_out_hbm.at[1], n_out.at[1])
-
-    slot_row = lax.broadcasted_iota(jnp.int32, (SLOTS, PEERS), 0)
-    spread = (slot_row // CAP == lax.broadcasted_iota(jnp.int32, (SLOTS, PEERS), 1)).astype(BF)
-    loads["list"].wait()
-    lists = lax.dot_general(
-        spread, list_ref[...].astype(F32).astype(BF), (((1,), (1,)), ((), ())), preferred_element_type=F32
-    )
-    own = lax.broadcasted_iota(jnp.int32, (SLOTS, CAP), 0) % CAP == lax.broadcasted_iota(
-        jnp.int32, (SLOTS, CAP), 1
-    )
-    chosen = jnp.sum(jnp.where(own, lists, 0.0), axis=1, keepdims=True).astype(jnp.int32)
-    pick[...] = (chosen == lax.broadcasted_iota(jnp.int32, (SLOTS, NODES), 1)).astype(BF)
-    for r in range(2):
-        rbuf[r, me] = jnp.zeros((16, 128), BF)
-
-    def project_and_pack(r):
-        loads[f"send{r}"].wait()
-        send_proj = dot(node_state[...], w_send[r]).astype(BF)
-        wcat[r, pl.ds(D + NODES, NODES), :] = send_proj
-        rows = dot(pick[...], send_proj)
-        for h in range(2):
-            first, second = swap_pairs(
-                rows[:, 256 * h : 256 * h + 128].reshape(PEERS // 2, 8, 128),
-                rows[:, 256 * h + 128 : 256 * h + 256].reshape(PEERS // 2, 8, 128),
-            )
-            part = jnp.stack([first, second], axis=1).reshape(PEERS, 8, 128)
-            if h == 0:
-                upper = part
-        sbuf[...] = jnp.concatenate([upper, part], axis=1).astype(BF)
-
-    def send(r, target):
-        pltpu.make_async_remote_copy(
-            src_ref=sbuf.at[target],
-            dst_ref=rbuf.at[r, me],
-            send_sem=ssem.at[r],
-            recv_sem=rsem.at[r],
-            device_id={"dom": target},
-            device_id_type=MESH,
-        ).start()
-
-    def send_far(r):
-        def body(j, carry):
-            plane = NX * NY - 1 - j
-            for dz in DZ_ORDER:
-                send(r, peer(lax.rem(plane, NX), dz, plane // NX))
-            return carry
-
-        lax.fori_loop(0, NX * NY - 1, body, 0)
-
-    def send_line(r):
-        for dz in DZ_ORDER:
-            send(r, peer(0, dz, 0))
-
-    def send_plane(r):
-        def body(plane, carry):
-            send(r, peer(lax.rem(plane, NX), 0, plane // NX))
-            return carry
-
-        lax.fori_loop(1, NX * NY, body, 0)
-
-    def receive(r):
-        everything = pltpu.make_async_remote_copy(
-            src_ref=sbuf.at[pl.ds(0, PEERS - 1)],
-            dst_ref=rbuf.at[r, pl.ds(0, PEERS - 1)],
-            send_sem=ssem.at[r],
-            recv_sem=rsem.at[r],
-            device_id={"dom": lax.rem(me + 1, PEERS)},
-            device_id_type=MESH,
-        )
-        everything.wait_send()
-        everything.wait_recv()
-        got = rbuf[r].astype(F32).reshape(PEERS // 2, 2, 2, 8, 128)
-        for h in range(2):
-            first, second = swap_pairs(got[:, 0, h], got[:, 1, h])
-            halo[:, 256 * h : 256 * h + 128] = first.reshape(SLOTS, 128).astype(BF)
-            halo[:, 256 * h + 128 : 256 * h + 256] = second.reshape(SLOTS, 128).astype(BF)
-
-    def tables():
-        senders = jnp.transpose(sender_ref[...])
-        receivers = jnp.transpose(receiver_ref[...])
-        masks = jnp.transpose(mask_ref[...])
-        nodes = lax.broadcasted_iota(jnp.int32, (128, NODES), 1)
-        slots = lax.broadcasted_iota(jnp.int32, (128, SLOTS), 1)
-        node_rows = lax.broadcasted_iota(jnp.int32, (NODES, 128), 0)
-        for j in range(EDGES // 128):
-            rows = pl.ds(j % 8 * 128, 128)
-            mask_col[pl.ds(j * 128, 128), :] = masks[:, j : j + 1].astype(F32)
-            received = (receivers[:, j : j + 1] == nodes).astype(BF)
-            if j < 8:
-                xl[rows, pl.ds(D, NODES)] = received
-                xl[rows, pl.ds(D + NODES, NODES)] = (senders[:, j : j + 1] == nodes).astype(BF)
-            else:
-                xr[rows, pl.ds(D, NODES)] = received
-                tr[rows, :] = (senders[:, j : j + 1] - NODES == slots).astype(BF)
-            live = jnp.where(mask_ref[j : j + 1, :] > 0, receiver_ref[j : j + 1, :], -1)
-            agg_t[:, pl.ds(j * 128, 128)] = (live == node_rows).astype(BF)
-
-    def local_edges(r):
-        def body(t, carry):
-            rows = pl.ds(pl.multiple_of(t * TILE, TILE), TILE)
-            hidden = dot(xl[rows, :], wcat[r]) + bias_ref[r, 0:1, :]
-            message, state = edge_tail(
-                hidden, xl[rows, pl.ds(0, D)], mask_col[rows, :],
-                w_out[r], bias_ref[r], gain_ref[r], shift_ref[r],
-            )
-            xl[rows, pl.ds(0, D)] = state
-            msg[rows, :] = message
-            return carry
-
-        lax.fori_loop(0, HALF // TILE, body, 0)
-        agg_acc[...] = dot(agg_t[:, pl.ds(0, HALF)], msg[...])
-
-    def remote_start(r):
-        def body(t, carry):
-            rows = pl.ds(pl.multiple_of(t * TILE, TILE), TILE)
-            hpre[rows, :] = dot(xr[rows, :], wcat[r, pl.ds(0, D + NODES), :]) + bias_ref[r, 0:1, :]
-            return carry
-
-        lax.fori_loop(0, HALF // TILE, body, 0)
-
-    loads["node"].wait()
-    project_and_pack(0)
-    pl.semaphore_wait(barrier, NZ - 1 + NX * NY - 1)
-    for plane in range(1, NX * NY):
-        tell(ready, peer(plane % NX, 0, plane // NX))
-    send_line(0)
-    pl.semaphore_wait(ready, NX * NY - 1)
+    pl.semaphore_wait(ready, NZ - 1)
     send_far(0)
     send_plane(0)
     for name in ("senders", "receivers", "masks", "biases", "gains", "shifts"):

time: 51 us -> 48.1 us (0.943)
  Pallas kernels: 50.1 us -> 47.2 us
    pallas_call x1, Pallas kernels: 5.31 us -> 3.57 us  [local(): pl.pallas_call(finish, out_shape=(pltpu.HBM((NODES, D), BF), pltpu.HBM((E...]
    pallas_call x1, Pallas kernels: 44.8 us -> 43.6 us  [local(): pl.pallas_call(kernel, out_shape=held, in_specs=[hbm] * 13, out_specs=(vm...]
where the time goes in v3:
time: 48.1 us; the launch traced here: 48 us
  Pallas kernels  47.2 us (98%)
  between operations  0.8 us (2%)
    pallas_call x1, Pallas kernels, local(): pl.pallas_call(kernel, out_shape=held, in_specs=[hbm] * 13, out_specs=(vm...  43.6 us
    pallas_call x1, Pallas kernels, local(): pl.pallas_call(finish, out_shape=(pltpu.HBM((NODES, D), BF), pltpu.HBM((E...  3.57 us

profile of v3, /device:TPU:2, one launch (start us, length us, event | category | flops | bytes accessed | tf_op | source)
XLA Modules:
  0.0 48.0 jit_solution(22910649369079753)
XLA Ops:
  0.6 43.6 %shard_map.140 = (bf16[1024,1024]{1,0:T(8,128)(2,1)S(1)}, bf16[1024,768]{1,0:T(8,128)(2,1)S(1)}, bf16[1024,512]{1,0:T(8,128)(2,1)S(1)}, bf16[256,2048]{1,0:T(8,1...) custom-call(bf16[256,512]{1,0:T(8,128)(2,1)} %node_hbm.1, ...), custom_call_target="tpu_custom_call" | custom-call | tf_op jit(solution)/shard_map/pallas_call | solution.py:342
  44.3 3.6 %shard_map.141 = (bf16[256,512]{1,0:T(8,128)(2,1)}, bf16[2048,512]{1,0:T(8,128)(2,1)}) custom-call(bf16[1024,1024]{1,0:T(8,128)(2,1)S(1)} %get-tuple-element.18.xl, bf16[1024,768]{1,0:T(8,128)(2,1)S(1)} %get-tuple-element.19.xr, bf16[1024,512]{1,0:T(8,128)(2,1)S(1)} %get-tuple-element.20.tr, bf16[256,2048]{1,0:T(8,128)(2,1)S(1)} %get-tuple-element.21.agg_t, ...), custom_call_target="tpu_custom_call" | custom-call | tf_op jit(solution)/shard_map/pallas_call | solution.py:368

commit v4 on v3

--- a/solution.py
+++ b/solution.py
@@ -13,7 +13,7 @@
 HALF = EDGES // 2
 SLOTS = PEERS * CAP
 NX, NZ, NY = 4, 8, 4
-TILE = 512
+TILE = 1024
 DZ_ORDER = (4, 3, 5, 2, 6, 1, 7)
 
 
@@ -38,6 +38,13 @@
     first = jnp.where(low, even, pltpu.roll(odd, 4, 1))
     second = jnp.where(low, pltpu.roll(even, 4, 1), odd)
     return first, second
+
+
+def slot_of(dx, dz, dy):
+    plane = dy * NX + dx
+    rank = jnp.where(dz < 4, 7 - 2 * dz, 2 * dz - 8)
+    near = jnp.where(dz == 0, plane, 16 + plane)
+    return jnp.where((dz == 0) | (dz == 4), near, 38 + plane * 6 - rank)
 
 
 def edge_tail(hidden, state, live, w_out, bias, gain, shift):
@@ -48,21 +55,20 @@
     return message, state + message
 
 
-def remote_edges(tr, halo, hpre, xr, mask_col, msg, state_ref, w_out, bias, gain, shift):
-    def body(t, carry):
-        rows = pl.ds(pl.multiple_of(t * TILE, TILE), TILE)
-        masks = mask_col[pl.ds(pl.multiple_of(HALF + t * TILE, TILE), TILE), :]
-        hidden = dot(tr[rows, :], halo[...]) + hpre[rows, :]
-        message, state = edge_tail(hidden, xr[rows, pl.ds(0, D)], masks, w_out, bias, gain, shift)
+def remote_edges(tr, halo, hpre, xr, mask_col, agg_t, agg_acc, state_ref, w_out, bias, gain, shift):
+    total = agg_acc[...]
+    for t in range(HALF // TILE):
+        rows, later = pl.ds(t * TILE, TILE), pl.ds(HALF + t * TILE, TILE)
+        hidden = dot(tr[rows, pl.ds(0, SLOTS // 2)], halo[pl.ds(0, SLOTS // 2), :]) + hpre[rows, :]
+        message, state = edge_tail(
+            hidden, xr[rows, pl.ds(0, D)], mask_col[later, :], w_out, bias, gain, shift
+        )
         state_ref[rows, pl.ds(0, D)] = state
-        msg[rows, :] = message
-        return carry
-
-    lax.fori_loop(0, HALF // TILE, body, 0, unroll=True)
-
-
-def node_step(agg_acc, agg_t, msg, nh_pre, node_state, w_in, w_out, bias, gain, shift):
-    total = (agg_acc[...] + dot(agg_t[:, pl.ds(HALF, HALF)], msg[...])).astype(BF)
+        total = total + dot(agg_t[:, later], message)
+    return total.astype(BF)
+
+
+def node_step(total, nh_pre, node_state, w_in, w_out, bias, gain, shift):
     act = silu(nh_pre[...] + dot(total, w_in)).astype(BF)
     projected = dot(act, w_out) + bias[3:4, :]
     update = layer_norm(projected, gain[1:2, :], shift[1:2, :])
@@ -74,9 +80,9 @@
     edge_in_hbm, edge_out_hbm, node_in_hbm, node_out_hbm, bias_hbm, gain_hbm, shift_hbm,
     xl, xr, tr, agg_t, hpre, halo, agg_acc, nh_pre, node_state, mask_col,
     w_out, n_in, n_out, bias_ref, gain_ref, shift_ref,
-    msg, wcat, w_send, w_recv, pick, sbuf, rbuf,
+    wcat, w_send, w_recv, pick, sbuf, rbuf, bundled,
     sender_ref, receiver_ref, mask_ref, list_ref,
-    ssem, rsem, ready, lsem,
+    ssem, rsem, bsem, ready, lsem,
 ):
     me = lax.axis_index("dom")
     x, z, y = lax.rem(me, NX), lax.rem(me // NX, NZ), me // (NX * NZ)
@@ -104,8 +110,9 @@
     for dz in range(1, NZ):
         tell(barrier, peer(0, dz, 0))
 
-    slot_row = lax.broadcasted_iota(jnp.int32, (SLOTS, PEERS), 0)
-    spread = (slot_row // CAP == lax.broadcasted_iota(jnp.int32, (SLOTS, PEERS), 1)).astype(BF)
+    p = lax.broadcasted_iota(jnp.int32, (1, PEERS), 1)
+    to = slot_of((p - x) & (NX - 1), ((p >> 2) - z) & (NZ - 1), ((p >> 5) - y) & (NY - 1))
+    spread = (lax.broadcasted_iota(jnp.int32, (SLOTS, PEERS), 0) // CAP == to).astype(BF)
     loads["list"].wait()
     lists = lax.dot_general(
         spread, list_ref[...].astype(F32).astype(BF), (((1,), (1,)), ((), ())), preferred_element_type=F32
@@ -116,7 +123,7 @@
     chosen = jnp.sum(jnp.where(own, lists, 0.0), axis=1, keepdims=True).astype(jnp.int32)
     pick[...] = (chosen == lax.broadcasted_iota(jnp.int32, (SLOTS, NODES), 1)).astype(BF)
     for r in range(2):
-        rbuf[r, me] = jnp.zeros((16, 128), BF)
+        rbuf[r, 0] = jnp.zeros((16, 128), BF)
 
     def project_and_pack(r):
         loads[f"send{r}"].wait()
@@ -133,55 +140,110 @@
                 upper = part
         sbuf[...] = jnp.concatenate([upper, part], axis=1).astype(BF)
 
-    def send(r, target):
+    def send(r, group, slot, target):
         pltpu.make_async_remote_copy(
-            src_ref=sbuf.at[target],
-            dst_ref=rbuf.at[r, me],
+            src_ref=sbuf.at[slot],
+            dst_ref=rbuf.at[r, slot],
             send_sem=ssem.at[r],
-            recv_sem=rsem.at[r],
+            recv_sem=rsem.at[r, group],
             device_id={"dom": target},
             device_id_type=MESH,
         ).start()
 
+    def send_off_plane(r, group, plane, ranks, opposite):
+        if opposite:
+            send(r, 1, 16 + plane, peer(lax.rem(plane, NX), 4, plane // NX))
+        for rank in ranks:
+            send(r, group, 38 + plane * 6 - rank, peer(lax.rem(plane, NX), DZ_ORDER[rank], plane // NX))
+
     def send_far(r):
-        def body(j, carry):
-            plane = NX * NY - 1 - j
-            for dz in DZ_ORDER:
-                send(r, peer(lax.rem(plane, NX), dz, plane // NX))
+        def first(j, carry):
+            send_off_plane(r, 0, 15 - j, range(1, 7), r == 1)
             return carry
 
-        lax.fori_loop(0, NX * NY - 1, body, 0)
+        def second(j, carry):
+            send_off_plane(r, 1, 4 - j, range(1, 7), r == 1)
+            return carry
+
+        lax.fori_loop(0, 10, first, 0)
+        send_off_plane(r, 0, 5, range(1, 5), r == 1)
+        send_off_plane(r, 1, 5, range(5, 7), False)
+        lax.fori_loop(0, 4, second, 0)
 
     def send_line(r):
-        for dz in DZ_ORDER:
-            send(r, peer(0, dz, 0))
+        send_off_plane(r, 1, 0, range(1, 7), r == 1)
+
+    def bundle():
+        return pltpu.make_async_remote_copy(
+            src_ref=sbuf.at[pl.ds(16, 16)],
+            dst_ref=bundled,
+            send_sem=bsem.at[0],
+            recv_sem=bsem.at[1],
+            device_id={"dom": peer(0, 4, 0)},
+            device_id_type=MESH,
+        )
+
+    def forward(plane):
+        return pltpu.make_async_remote_copy(
+            src_ref=bundled.at[plane],
+            dst_ref=rbuf.at[0, 16 + plane],
+            send_sem=bsem.at[2],
+            recv_sem=rsem.at[0, 1],
+            device_id={"dom": peer(lax.rem(plane, NX), 0, plane // NX)},
+            device_id_type=MESH,
+        )
+
+    def forward_bundle():
+        bundle().wait()
+
+        def body(plane, carry):
+            forward(plane).start()
+            return carry
+
+        lax.fori_loop(1, NX * NY, body, 0)
+        rbuf[0, 16] = bundled[0]
 
     def send_plane(r):
         def body(plane, carry):
-            send(r, peer(lax.rem(plane, NX), 0, plane // NX))
+            send(r, 1, plane, peer(lax.rem(plane, NX), 0, plane // NX))
             return carry
 
         lax.fori_loop(1, NX * NY, body, 0)
 
-    def receive(r):
-        everything = pltpu.make_async_remote_copy(
-            src_ref=sbuf.at[pl.ds(0, PEERS - 1)],
-            dst_ref=rbuf.at[r, pl.ds(0, PEERS - 1)],
+    def arrived(r, first, count, group):
+        return pltpu.make_async_remote_copy(
+            src_ref=sbuf.at[pl.ds(first, count)],
+            dst_ref=rbuf.at[r, pl.ds(first, count)],
             send_sem=ssem.at[r],
-            recv_sem=rsem.at[r],
+            recv_sem=rsem.at[r, group],
             device_id={"dom": lax.rem(me + 1, PEERS)},
             device_id_type=MESH,
         )
-        everything.wait_send()
-        everything.wait_recv()
-        got = rbuf[r].astype(F32).reshape(PEERS // 2, 2, 2, 8, 128)
+
+    def receive(r, group):
+        if group == 0:
+            arrived(r, 64, 64, 0).wait_recv()
+        else:
+            arrived(r, 1, 63 - (r == 0), 1).wait_recv()
+        first, rows = (1 - group) * 64, SLOTS // 2
+        got = rbuf[r, pl.ds(first, 64)].astype(F32).reshape(32, 2, 2, 8, 128)
         for h in range(2):
-            first, second = swap_pairs(got[:, 0, h], got[:, 1, h])
-            halo[:, 256 * h : 256 * h + 128] = first.reshape(SLOTS, 128).astype(BF)
-            halo[:, 256 * h + 128 : 256 * h + 256] = second.reshape(SLOTS, 128).astype(BF)
+            left, right = swap_pairs(got[:, 0, h], got[:, 1, h])
+            at = pl.ds(first * CAP, rows)
+            halo[at, 256 * h : 256 * h + 128] = left.reshape(rows, 128).astype(BF)
+            halo[at, 256 * h + 128 : 256 * h + 256] = right.reshape(rows, 128).astype(BF)
+
+    def remote_half(r):
+        for t in range(HALF // TILE):
+            rows, late = pl.ds(t * TILE, TILE), pl.ds(SLOTS // 2, SLOTS // 2)
+            hpre[rows, :] = hpre[rows, :] + dot(tr[rows, late], halo[late, :])
 
     def tables():
-        senders = jnp.transpose(sender_ref[...])
+        far = sender_ref[...] - NODES
+        at = slot_of(
+            (x - (far >> 2)) & (NX - 1), (z - (far >> 4)) & (NZ - 1), (y - (far >> 7)) & (NY - 1)
+        )
+        senders = jnp.transpose(jnp.where(far >= 0, at * CAP + (far & (CAP - 1)), sender_ref[...]))
         receivers = jnp.transpose(receiver_ref[...])
         masks = jnp.transpose(mask_ref[...])
         nodes = lax.broadcasted_iota(jnp.int32, (128, NODES), 1)
@@ -196,38 +258,34 @@
                 xl[rows, pl.ds(D + NODES, NODES)] = (senders[:, j : j + 1] == nodes).astype(BF)
             else:
                 xr[rows, pl.ds(D, NODES)] = received
-                tr[rows, :] = (senders[:, j : j + 1] - NODES == slots).astype(BF)
+                tr[rows, :] = (senders[:, j : j + 1] == slots).astype(BF)
             live = jnp.where(mask_ref[j : j + 1, :] > 0, receiver_ref[j : j + 1, :], -1)
             agg_t[:, pl.ds(j * 128, 128)] = (live == node_rows).astype(BF)
 
     def local_edges(r):
-        def body(t, carry):
-            rows = pl.ds(pl.multiple_of(t * TILE, TILE), TILE)
+        total = jnp.zeros((NODES, D), F32)
+        for t in range(HALF // TILE):
+            rows = pl.ds(t * TILE, TILE)
             hidden = dot(xl[rows, :], wcat[r]) + bias_ref[r, 0:1, :]
             message, state = edge_tail(
                 hidden, xl[rows, pl.ds(0, D)], mask_col[rows, :],
                 w_out[r], bias_ref[r], gain_ref[r], shift_ref[r],
             )
             xl[rows, pl.ds(0, D)] = state
-            msg[rows, :] = message
-            return carry
-
-        lax.fori_loop(0, HALF // TILE, body, 0, unroll=True)
-        agg_acc[...] = dot(agg_t[:, pl.ds(0, HALF)], msg[...])
+            total = total + dot(agg_t[:, rows], message)
+        agg_acc[...] = total
 
     def remote_start(r):
-        def body(t, carry):
-            rows = pl.ds(pl.multiple_of(t * TILE, TILE), TILE)
+        for t in range(HALF // TILE):
+            rows = pl.ds(t * TILE, TILE)
             hpre[rows, :] = dot(xr[rows, :], wcat[r, pl.ds(0, D + NODES), :]) + bias_ref[r, 0:1, :]
-            return carry
-
-        lax.fori_loop(0, HALF // TILE, body, 0, unroll=True)
 
     loads["node"].wait()
     project_and_pack(0)
     pl.semaphore_wait(barrier, NZ - 1 + NX * NY - 1)
     for dz in range(1, NZ):
         tell(ready, peer(0, dz, 0))
+    bundle().start()
     send_line(0)
     load("senders", sender_hbm, sender_ref)
     load("receivers", receiver_hbm, receiver_ref)
@@ -250,6 +308,7 @@
     load("nout1", node_out_hbm.at[1], n_out.at[1])
     pl.semaphore_wait(ready, NZ - 1)
     send_far(0)
+    forward_bundle()
     send_plane(0)
     for name in ("senders", "receivers", "masks", "biases", "gains", "shifts"):
         loads[name].wait()
@@ -268,14 +327,26 @@
         loads[f"nin{r}"].wait()
         loads[f"nout{r}"].wait()
         nh_pre[...] = dot(node_state[...], n_in[r, 0]) + bias_ref[r, 2:3, :]
-        receive(r)
+        receive(r, 0)
+        remote_half(r)
+        arrived(r, 0, 111 if r == 0 else 127, 0).wait_send()
         if r == 0:
-            remote_edges(
-                tr, halo, hpre, xr, mask_col, msg, xr,
+            pltpu.make_async_remote_copy(
+                src_ref=bundled.at[pl.ds(1, 15)],
+                dst_ref=rbuf.at[0, pl.ds(1, 15)],
+                send_sem=bsem.at[2],
+                recv_sem=rsem.at[0, 1],
+                device_id={"dom": lax.rem(me + 1, PEERS)},
+                device_id_type=MESH,
+            ).wait_send()
+        receive(r, 1)
+        if r == 0:
+            total = remote_edges(
+                tr, halo, hpre, xr, mask_col, agg_t, agg_acc, xr,
                 w_out[r], bias_ref[r], gain_ref[r], shift_ref[r],
             )
             node_state[...] = node_step(
-                agg_acc, agg_t, msg, nh_pre, node_state,
+                total, nh_pre, node_state,
                 n_in[r, 1], n_out[r], bias_ref[r], gain_ref[r], shift_ref[r],
             )
             project_and_pack(1)
@@ -288,18 +359,18 @@
     xl, xr, tr, agg_t, hpre, halo, agg_acc, nh_pre, node_state, mask_col,
     w_out, n_in, n_out, bias_ref, gain_ref, shift_ref,
     node_out_hbm, edge_out_hbm,
-    msg, state, node_new, osem,
+    state, node_new, osem,
 ):
     near = pltpu.make_async_copy(xl.at[:, pl.ds(0, D)], edge_out_hbm.at[pl.ds(0, HALF)], osem.at[0])
     near.start()
-    remote_edges(
-        tr, halo, hpre, xr, mask_col, msg, state,
+    total = remote_edges(
+        tr, halo, hpre, xr, mask_col, agg_t, agg_acc, state,
         w_out[1], bias_ref[1], gain_ref[1], shift_ref[1],
     )
     far = pltpu.make_async_copy(state, edge_out_hbm.at[pl.ds(HALF, HALF)], osem.at[1])
     far.start()
     node_new[...] = node_step(
-        agg_acc, agg_t, msg, nh_pre, node_state,
+        total, nh_pre, node_state,
         n_in[1, 1], n_out[1], bias_ref[1], gain_ref[1], shift_ref[1],
     )
     nodes = pltpu.make_async_copy(node_new, node_out_hbm, osem.at[2])
@@ -345,19 +416,20 @@
         in_specs=[hbm] * 13,
         out_specs=(vmem,) * len(held),
         scratch_shapes=[
-            pltpu.VMEM((HALF, D), BF),
             pltpu.VMEM((2, D + 2 * NODES, D), BF),
             pltpu.VMEM((2, D, D), BF),
             pltpu.VMEM((2, D, D), BF),
             pltpu.VMEM((SLOTS, NODES), BF),
             pltpu.VMEM((PEERS, 16, 128), BF),
             pltpu.VMEM((2, PEERS, 16, 128), BF),
+            pltpu.VMEM((16, 16, 128), BF),
             pltpu.VMEM((16, 128), jnp.int32),
             pltpu.VMEM((16, 128), jnp.int32),
             pltpu.VMEM((16, 128), jnp.int32),
             pltpu.VMEM((CAP, PEERS), jnp.int32),
             pltpu.SemaphoreType.DMA((2,)),
-            pltpu.SemaphoreType.DMA((2,)),
+            pltpu.SemaphoreType.DMA((2, 2)),
+            pltpu.SemaphoreType.DMA((3,)),
             pltpu.SemaphoreType.REGULAR,
             pltpu.SemaphoreType.DMA((22,)),
         ],
@@ -372,7 +444,6 @@
         out_specs=(hbm, hbm),
         scratch_shapes=[
             pltpu.VMEM((HALF, D), BF),
-            pltpu.VMEM((HALF, D), BF),
             pltpu.VMEM((NODES, D), BF),
             pltpu.SemaphoreType.DMA((3,)),
         ],

time: 48.1 us -> 47.3 us (0.983); the launches traced: 48 us -> 46.7 us
  Pallas kernels: 47.2 us -> 45.9 us
    pallas_call x1, Pallas kernels: 43.6 us -> 42.4 us  [local(): pl.pallas_call(kernel, out_shape=held, in_specs=[hbm] * 13, out_specs=(vm...]
where the time goes in v4:
time: 47.3 us; the launch traced here: 46.7 us
  Pallas kernels  45.9 us (97%)
  between operations  0.8 us (2%)
    pallas_call x1, Pallas kernels, local(): pl.pallas_call(kernel, out_shape=held, in_specs=[hbm] * 13, out_specs=(vm...  42.4 us
    pallas_call x1, Pallas kernels, local(): pl.pallas_call(finish, out_shape=(pltpu.HBM((NODES, D), BF), pltpu.HBM((E...  3.45 us

profile of v4, /device:TPU:2, one launch (start us, length us, event | category | flops | bytes accessed | tf_op | source)
XLA Modules:
  0.0 46.7 jit_solution(6188222524652212705)
XLA Ops:
  0.6 42.4 %shard_map.140 = (bf16[1024,1024]{1,0:T(8,128)(2,1)S(1)}, bf16[1024,768]{1,0:T(8,128)(2,1)S(1)}, bf16[1024,512]{1,0:T(8,128)(2,1)S(1)}, bf16[256,2048]{1,0:T(8,1...) custom-call(bf16[256,512]{1,0:T(8,128)(2,1)} %node_hbm.1, ...), custom_call_target="tpu_custom_call" | custom-call | tf_op jit(solution)/shard_map/pallas_call | solution.py:413
  43.0 3.4 %shard_map.141 = (bf16[256,512]{1,0:T(8,128)(2,1)}, bf16[2048,512]{1,0:T(8,128)(2,1)}) custom-call(bf16[1024,1024]{1,0:T(8,128)(2,1)S(1)} %get-tuple-element.18.xl, bf16[1024,768]{1,0:T(8,128)(2,1)S(1)} %get-tuple-element.19.xr, bf16[1024,512]{1,0:T(8,128)(2,1)S(1)} %get-tuple-element.20.tr, bf16[256,2048]{1,0:T(8,128)(2,1)S(1)} %get-tuple-element.21.agg_t, ...), custom_call_target="tpu_custom_call" | custom-call | tf_op jit(solution)/shard_map/pallas_call | solution.py:440

commit v5 on v4

--- a/solution.py
+++ b/solution.py
@@ -103,6 +103,9 @@
     load("list", list_hbm, list_ref)
     load("node", node_hbm, node_state)
     load("send0", edge_in_hbm.at[0, 1], w_send.at[0])
+    load("senders", sender_hbm, sender_ref)
+    load("receivers", receiver_hbm, receiver_ref)
+    load("masks", mask_hbm, mask_ref)
 
     barrier = pltpu.get_barrier_semaphore()
     for plane in range(1, NX * NY):
@@ -287,9 +290,6 @@
         tell(ready, peer(0, dz, 0))
     bundle().start()
     send_line(0)
-    load("senders", sender_hbm, sender_ref)
-    load("receivers", receiver_hbm, receiver_ref)
-    load("masks", mask_hbm, mask_ref)
     load("biases", bias_hbm, bias_ref)
     load("gains", gain_hbm, gain_ref)
     load("shifts", shift_hbm, shift_ref)
@@ -306,13 +306,15 @@
     load("out1", edge_out_hbm.at[1], w_out.at[1])
     load("nin1", node_in_hbm.at[1], n_in.at[1])
     load("nout1", node_out_hbm.at[1], n_out.at[1])
+    for name in ("senders", "receivers", "masks"):
+        loads[name].wait()
+    tables()
     pl.semaphore_wait(ready, NZ - 1)
     send_far(0)
     forward_bundle()
     send_plane(0)
-    for name in ("senders", "receivers", "masks", "biases", "gains", "shifts"):
+    for name in ("biases", "gains", "shifts"):
         loads[name].wait()
-    tables()
 
     for r in range(2):
         loads[f"recv{r}"].wait()

time: 47.3 us -> 47.3 us (level)
  no operation moved by 1% of the time
where the time goes in v5:
time: 47.3 us; the launch traced here: 46.6 us
  Pallas kernels  45.8 us (97%)
  between operations  0.8 us (2%)
    pallas_call x1, Pallas kernels, local(): pl.pallas_call(kernel, out_shape=held, in_specs=[hbm] * 13, out_specs=(vm...  42.4 us
    pallas_call x1, Pallas kernels, local(): pl.pallas_call(finish, out_shape=(pltpu.HBM((NODES, D), BF), pltpu.HBM((E...  3.45 us

profile of v5, /device:TPU:2, one launch (start us, length us, event | category | flops | bytes accessed | tf_op | source)
XLA Modules:
  0.0 46.6 jit_solution(12465069364073643461)
XLA Ops:
  0.6 42.4 %shard_map.140 = (bf16[1024,1024]{1,0:T(8,128)(2,1)S(1)}, bf16[1024,768]{1,0:T(8,128)(2,1)S(1)}, bf16[1024,512]{1,0:T(8,128)(2,1)S(1)}, bf16[256,2048]{1,0:T(8,1...) custom-call(bf16[256,512]{1,0:T(8,128)(2,1)} %node_hbm.1, ...), custom_call_target="tpu_custom_call" | custom-call | tf_op jit(solution)/shard_map/pallas_call | solution.py:415
  43.0 3.5 %shard_map.141 = (bf16[256,512]{1,0:T(8,128)(2,1)}, bf16[2048,512]{1,0:T(8,128)(2,1)}) custom-call(bf16[1024,1024]{1,0:T(8,128)(2,1)S(1)} %get-tuple-element.18.xl, bf16[1024,768]{1,0:T(8,128)(2,1)S(1)} %get-tuple-element.19.xr, bf16[1024,512]{1,0:T(8,128)(2,1)S(1)} %get-tuple-element.20.tr, bf16[256,2048]{1,0:T(8,128)(2,1)S(1)} %get-tuple-element.21.agg_t, ...), custom_call_target="tpu_custom_call" | custom-call | tf_op jit(solution)/shard_map/pallas_call | solution.py:442

commit v6 on v5

--- a/solution.py
+++ b/solution.py
@@ -43,12 +43,12 @@
 def slot_of(dx, dz, dy):
     plane = dy * NX + dx
     rank = jnp.where(dz < 4, 7 - 2 * dz, 2 * dz - 8)
-    near = jnp.where(dz == 0, plane, 16 + plane)
-    return jnp.where((dz == 0) | (dz == 4), near, 38 + plane * 6 - rank)
+    off_plane = jnp.where(rank < 2, 16 + 16 * rank + plane, 54 + plane * 5 - rank)
+    return jnp.where(dz == 0, plane, off_plane)
 
 
 def edge_tail(hidden, state, live, w_out, bias, gain, shift):
-    act = silu(hidden).astype(BF)
+    act = silu(hidden.astype(BF))
     projected = dot(act, w_out) + bias[1:2, :]
     message = layer_norm(projected, gain[0:1, :], shift[0:1, :])
     message = jnp.where(live > 0, message, 0.0).astype(BF)
@@ -153,58 +153,59 @@
             device_id_type=MESH,
         ).start()
 
-    def send_off_plane(r, group, plane, ranks, opposite):
-        if opposite:
-            send(r, 1, 16 + plane, peer(lax.rem(plane, NX), 4, plane // NX))
+    def send_off_plane(r, group, plane, ranks):
         for rank in ranks:
-            send(r, group, 38 + plane * 6 - rank, peer(lax.rem(plane, NX), DZ_ORDER[rank], plane // NX))
+            slot = 16 + 16 * rank + plane if rank < 2 else 54 + plane * 5 - rank
+            send(
+                r, 1 if rank < 2 else group, slot,
+                peer(lax.rem(plane, NX), DZ_ORDER[rank], plane // NX),
+            )
 
     def send_far(r):
+        start = 2 * (r == 0)
+
         def first(j, carry):
-            send_off_plane(r, 0, 15 - j, range(1, 7), r == 1)
+            send_off_plane(r, 0, 15 - j, range(start, 7))
             return carry
 
         def second(j, carry):
-            send_off_plane(r, 1, 4 - j, range(1, 7), r == 1)
+            send_off_plane(r, 1, 2 - j, range(start, 7))
             return carry
 
-        lax.fori_loop(0, 10, first, 0)
-        send_off_plane(r, 0, 5, range(1, 5), r == 1)
-        send_off_plane(r, 1, 5, range(5, 7), False)
-        lax.fori_loop(0, 4, second, 0)
+        lax.fori_loop(0, 12, first, 0)
+        send_off_plane(r, 0, 3, range(start, 6))
+        send_off_plane(r, 1, 3, range(6, 7))
+        lax.fori_loop(0, 2, second, 0)
 
     def send_line(r):
-        send_off_plane(r, 1, 0, range(1, 7), r == 1)
-
-    def bundle():
+        send_off_plane(r, 1, 0, range(2 * (r == 0), 7))
+
+    def bundle(k):
         return pltpu.make_async_remote_copy(
-            src_ref=sbuf.at[pl.ds(16, 16)],
-            dst_ref=bundled,
-            send_sem=bsem.at[0],
-            recv_sem=bsem.at[1],
-            device_id={"dom": peer(0, 4, 0)},
+            src_ref=sbuf.at[pl.ds(16 + 16 * k, 16)],
+            dst_ref=bundled.at[k],
+            send_sem=bsem.at[0, k],
+            recv_sem=bsem.at[1, k],
+            device_id={"dom": peer(0, DZ_ORDER[k], 0)},
             device_id_type=MESH,
         )
 
-    def forward(plane):
-        return pltpu.make_async_remote_copy(
-            src_ref=bundled.at[plane],
-            dst_ref=rbuf.at[0, 16 + plane],
-            send_sem=bsem.at[2],
-            recv_sem=rsem.at[0, 1],
-            device_id={"dom": peer(lax.rem(plane, NX), 0, plane // NX)},
-            device_id_type=MESH,
-        )
-
-    def forward_bundle():
-        bundle().wait()
+    def forward_bundle(k):
+        bundle(k).wait()
 
         def body(plane, carry):
-            forward(plane).start()
+            pltpu.make_async_remote_copy(
+                src_ref=bundled.at[k, plane],
+                dst_ref=rbuf.at[0, 16 + 16 * k + plane],
+                send_sem=bsem.at[2, k],
+                recv_sem=rsem.at[0, 1],
+                device_id={"dom": peer(lax.rem(plane, NX), 0, plane // NX)},
+                device_id_type=MESH,
+            ).start()
             return carry
 
         lax.fori_loop(1, NX * NY, body, 0)
-        rbuf[0, 16] = bundled[0]
+        rbuf[0, 16 + 16 * k] = bundled[k, 0]
 
     def send_plane(r):
         def body(plane, carry):
@@ -227,7 +228,7 @@
         if group == 0:
             arrived(r, 64, 64, 0).wait_recv()
         else:
-            arrived(r, 1, 63 - (r == 0), 1).wait_recv()
+            arrived(r, 1, 63 - 2 * (r == 0), 1).wait_recv()
         first, rows = (1 - group) * 64, SLOTS // 2
         got = rbuf[r, pl.ds(first, 64)].astype(F32).reshape(32, 2, 2, 8, 128)
         for h in range(2):
@@ -288,7 +289,8 @@
     pl.semaphore_wait(barrier, NZ - 1 + NX * NY - 1)
     for dz in range(1, NZ):
         tell(ready, peer(0, dz, 0))
-    bundle().start()
+    for k in range(2):
+        bundle(k).start()
     send_line(0)
     load("biases", bias_hbm, bias_ref)
     load("gains", gain_hbm, gain_ref)
@@ -311,7 +313,8 @@
     tables()
     pl.semaphore_wait(ready, NZ - 1)
     send_far(0)
-    forward_bundle()
+    for k in range(2):
+        forward_bundle(k)
     send_plane(0)
     for name in ("biases", "gains", "shifts"):
         loads[name].wait()
@@ -331,16 +334,17 @@
         nh_pre[...] = dot(node_state[...], n_in[r, 0]) + bias_ref[r, 2:3, :]
         receive(r, 0)
         remote_half(r)
-        arrived(r, 0, 111 if r == 0 else 127, 0).wait_send()
+        arrived(r, 0, 95 if r == 0 else 127, 0).wait_send()
         if r == 0:
-            pltpu.make_async_remote_copy(
-                src_ref=bundled.at[pl.ds(1, 15)],
-                dst_ref=rbuf.at[0, pl.ds(1, 15)],
-                send_sem=bsem.at[2],
-                recv_sem=rsem.at[0, 1],
-                device_id={"dom": lax.rem(me + 1, PEERS)},
-                device_id_type=MESH,
-            ).wait_send()
+            for k in range(2):
+                pltpu.make_async_remote_copy(
+                    src_ref=bundled.at[k, pl.ds(1, 15)],
+                    dst_ref=rbuf.at[0, pl.ds(1, 15)],
+                    send_sem=bsem.at[2, k],
+                    recv_sem=rsem.at[0, 1],
+                    device_id={"dom": lax.rem(me + 1, PEERS)},
+                    device_id_type=MESH,
+                ).wait_send()
         receive(r, 1)
         if r == 0:
             total = remote_edges(
@@ -424,14 +428,14 @@
             pltpu.VMEM((SLOTS, NODES), BF),
             pltpu.VMEM((PEERS, 16, 128), BF),
             pltpu.VMEM((2, PEERS, 16, 128), BF),
-            pltpu.VMEM((16, 16, 128), BF),
+            pltpu.VMEM((2, 16, 16, 128), BF),
             pltpu.VMEM((16, 128), jnp.int32),
             pltpu.VMEM((16, 128), jnp.int32),
             pltpu.VMEM((16, 128), jnp.int32),
             pltpu.VMEM((CAP, PEERS), jnp.int32),
             pltpu.SemaphoreType.DMA((2,)),
             pltpu.SemaphoreType.DMA((2, 2)),
-            pltpu.SemaphoreType.DMA((3,)),
+            pltpu.SemaphoreType.DMA((3, 2)),
             pltpu.SemaphoreType.REGULAR,
             pltpu.SemaphoreType.DMA((22,)),
         ],

time: 47.3 us -> 47.2 us (level)
  no operation moved by 1% of the time
where the time goes in v6:
time: 47.2 us; the launch traced here: 46.4 us
  Pallas kernels  45.6 us (97%)
  between operations  0.8 us (2%)
    pallas_call x1, Pallas kernels, local(): pl.pallas_call(kernel, out_shape=held, in_specs=[hbm] * 13, out_specs=(vm...  42.3 us
    pallas_call x1, Pallas kernels, local(): pl.pallas_call(finish, out_shape=(pltpu.HBM((NODES, D), BF), pltpu.HBM((E...  3.3 us

profile of v6, /device:TPU:2, one launch (start us, length us, event | category | flops | bytes accessed | tf_op | source)
XLA Modules:
  0.0 46.4 jit_solution(12077066694203359677)
XLA Ops:
  0.6 42.3 %shard_map.140 = (bf16[1024,1024]{1,0:T(8,128)(2,1)S(1)}, bf16[1024,768]{1,0:T(8,128)(2,1)S(1)}, bf16[1024,512]{1,0:T(8,128)(2,1)S(1)}, bf16[256,2048]{1,0:T(8,1...) custom-call(bf16[256,512]{1,0:T(8,128)(2,1)} %node_hbm.1, ...), custom_call_target="tpu_custom_call" | custom-call | tf_op jit(solution)/shard_map/pallas_call | solution.py:419
  42.9 3.3 %shard_map.141 = (bf16[256,512]{1,0:T(8,128)(2,1)}, bf16[2048,512]{1,0:T(8,128)(2,1)}) custom-call(bf16[1024,1024]{1,0:T(8,128)(2,1)S(1)} %get-tuple-element.18.xl, bf16[1024,768]{1,0:T(8,128)(2,1)S(1)} %get-tuple-element.19.xr, bf16[1024,512]{1,0:T(8,128)(2,1)S(1)} %get-tuple-element.20.tr, bf16[256,2048]{1,0:T(8,128)(2,1)S(1)} %get-tuple-element.21.agg_t, ...), custom_call_target="tpu_custom_call" | custom-call | tf_op jit(solution)/shard_map/pallas_call | solution.py:446

commit v7 on v4

--- a/solution.py
+++ b/solution.py
@@ -48,7 +48,7 @@
 
 
 def edge_tail(hidden, state, live, w_out, bias, gain, shift):
-    act = silu(hidden).astype(BF)
+    act = silu(hidden.astype(BF))
     projected = dot(act, w_out) + bias[1:2, :]
     message = layer_norm(projected, gain[0:1, :], shift[0:1, :])
     message = jnp.where(live > 0, message, 0.0).astype(BF)

time: 47.3 us -> 47 us (level)
  no operation moved by 1% of the time
where the time goes in v7:
time: 47 us; the launch traced here: 46.4 us
  Pallas kernels  45.6 us (97%)
  between operations  0.8 us (2%)
    pallas_call x1, Pallas kernels, local(): pl.pallas_call(kernel, out_shape=held, in_specs=[hbm] * 13, out_specs=(vm...  42.3 us
    pallas_call x1, Pallas kernels, local(): pl.pallas_call(finish, out_shape=(pltpu.HBM((NODES, D), BF), pltpu.HBM((E...  3.3 us

profile of v7, /device:TPU:2, one launch (start us, length us, event | category | flops | bytes accessed | tf_op | source)
XLA Modules:
  0.0 46.4 jit_solution(13890128457898707846)
XLA Ops:
  0.6 42.3 %shard_map.140 = (bf16[1024,1024]{1,0:T(8,128)(2,1)S(1)}, bf16[1024,768]{1,0:T(8,128)(2,1)S(1)}, bf16[1024,512]{1,0:T(8,128)(2,1)S(1)}, bf16[256,2048]{1,0:T(8,1...) custom-call(bf16[256,512]{1,0:T(8,128)(2,1)} %node_hbm.1, ...), custom_call_target="tpu_custom_call" | custom-call | tf_op jit(solution)/shard_map/pallas_call | solution.py:413
  42.9 3.3 %shard_map.141 = (bf16[256,512]{1,0:T(8,128)(2,1)}, bf16[2048,512]{1,0:T(8,128)(2,1)}) custom-call(bf16[1024,1024]{1,0:T(8,128)(2,1)S(1)} %get-tuple-element.18.xl, bf16[1024,768]{1,0:T(8,128)(2,1)S(1)} %get-tuple-element.19.xr, bf16[1024,512]{1,0:T(8,128)(2,1)S(1)} %get-tuple-element.20.tr, bf16[256,2048]{1,0:T(8,128)(2,1)S(1)} %get-tuple-element.21.agg_t, ...), custom_call_target="tpu_custom_call" | custom-call | tf_op jit(solution)/shard_map/pallas_call | solution.py:440
